TPU v7x, 32 devices: a whole 2x2x4 slice. The times are simulated.
32 devices in a mesh: segment: 4 (over y, x), ctx: 8 (over z, core).
Axes of the slice: x: 2, y: 2, z: 4, core: 2. Of those that a mesh axis runs over, the one named last changes fastest.
Arguments:
- queries: bfloat16 [4, 8, 2048, 2048], P('segment', None, 'ctx'), may hold values from -3 to 3
- keys: bfloat16 [4, 8, 2048, 512], P('segment', None, 'ctx'), may hold values from -3 to 3
- values: bfloat16 [4, 8, 2048, 512], P('segment', None, 'ctx'), may hold values from -6 to 6
- grad_slab: bfloat16 [4, 2048, 2048], P('segment', 'ctx'), may hold values from -6 to 6
- plan: int32 [4], P('segment'), may hold values from 0 to 7
- random_blocks: int32 [16, 3], replicated, may hold values from 1 to 15, as said below
Outputs:
- query_grad: bfloat16 [4, 2048, 2048], P('segment', 'ctx')
- key_grad: bfloat16 [4, 2048, 512], P('segment', 'ctx')
- value_grad: bfloat16 [4, 2048, 512], P('segment', 'ctx')
Inputs may be any that keep to these rules, and one draw needn't show every extreme that they name: `random_blocks`: each row b holds 3 different block numbers, none equal to b - 1, b, b + 1 (mod 16) or to 0.
All inputs are finite; a program needn't handle non-finite values.
Results may differ from a plain program's by a relative error of at most 0.012.
Values may be sent and summed in bfloat16 or wider, within the bound.
A program may use at most 192 MiB of HBM per device.

v0:
```python
import jax
import jax.numpy as jnp
from jax import lax
from jax.sharding import PartitionSpec as P

HD = 128
BLK = 128


def from_behind(block, axis, distance):
    devices = range(lax.axis_size(axis))
    route = [((i - distance) % len(devices), i) for i in devices]
    return lax.ppermute(block, axis, route)


def unchanged(partial_sum):
    return partial_sum


def global_rows(query_rows, grad_rows, key_set, value_set, score_scale, total_fn, delta_fn):
    scores = (
        jnp.einsum("htgd,hsd->hgts", query_rows, key_set, preferred_element_type=jnp.float32)
        * score_scale
    )
    exp_scores = jnp.exp(scores)
    totals = total_fn(jnp.sum(exp_scores, axis=3))
    weights = exp_scores / totals[..., None]
    weights_low = weights.astype(jnp.bfloat16)
    dprobs = jnp.einsum("htgd,hsd->hgts", grad_rows, value_set, preferred_element_type=jnp.float32)
    deltas = delta_fn(jnp.sum(weights_low.astype(jnp.float32) * dprobs, axis=3))
    dscore = (weights * (dprobs - deltas[..., None])).astype(jnp.bfloat16)
    dquery = score_scale * jnp.einsum(
        "hgts,hsd->htgd", dscore, key_set, preferred_element_type=jnp.float32
    )
    key_term = score_scale * jnp.einsum(
        "hgts,htgd->hsd", dscore, query_rows, preferred_element_type=jnp.float32
    )
    value_term = jnp.einsum(
        "hgts,htgd->hsd", weights_low, grad_rows, preferred_element_type=jnp.float32
    )
    return (dquery, key_term, value_term)


def per_device(queries, keys, values, grad_slab, plan, random_blocks):
    upstream = from_behind(grad_slab, "segment", -1)[0]
    chosen_mb = plan[0]
    query_now = lax.dynamic_index_in_dim(queries[0], chosen_mb, 0, keepdims=False)
    key_now = lax.dynamic_index_in_dim(keys[0], chosen_mb, 0, keepdims=False)
    value_now = lax.dynamic_index_in_dim(values[0], chosen_mb, 0, keepdims=False)
    tok_rows = query_now.shape[0]
    q_width = query_now.shape[1]
    kv_width = key_now.shape[1]
    kv_heads = kv_width // HD
    group_size = q_width // HD // kv_heads
    n_local = tok_rows // BLK
    n_blocks = n_local * lax.axis_size("ctx")
    score_scale = HD ** (-0.5)
    key_all, value_all = (
        lax.all_gather(key_now, "ctx", axis=0, tiled=True),
        lax.all_gather(value_now, "ctx", axis=0, tiled=True),
    )
    first_block = lax.axis_index("ctx") * n_local
    my_blocks = first_block + jnp.arange(n_local, dtype=jnp.int32)
    global_id = jnp.int32(0)
    rand_rows = lax.dynamic_slice_in_dim(random_blocks, first_block, n_local, 0)
    window_ids = jnp.stack(
        [(my_blocks - 1) % n_blocks, my_blocks, (my_blocks + 1) % n_blocks], axis=1
    )
    in_window = jnp.any(window_ids == global_id, axis=1)
    slot_ids = jnp.concatenate([window_ids, jnp.zeros((n_local, 1), jnp.int32), rand_rows], axis=1)
    n_slots = slot_ids.shape[1]
    valid_slots = jnp.concatenate(
        [
            jnp.ones((n_local, 3), jnp.float32),
            (1.0 - in_window.astype(jnp.float32))[:, None],
            jnp.ones((n_local, n_slots - 4), jnp.float32),
        ],
        axis=1,
    )
    plain_row = (my_blocks != global_id).astype(jnp.float32).reshape(n_local, 1, 1, 1, 1, 1)
    query_five = query_now.reshape(n_local, BLK, kv_heads, group_size, HD)
    grad_five = upstream.reshape(n_local, BLK, kv_heads, group_size, HD)
    key_blocks = key_all.reshape(n_blocks, BLK, kv_heads, HD)[slot_ids]
    value_blocks = value_all.reshape(n_blocks, BLK, kv_heads, HD)[slot_ids]
    scores = (
        jnp.einsum(
            "ntkgd,neskd->nkgtes", query_five, key_blocks, preferred_element_type=jnp.float32
        )
        * score_scale
    )
    exp_scores = jnp.exp(scores) * valid_slots.reshape(n_local, 1, 1, 1, n_slots, 1)
    totals = jnp.sum(exp_scores, axis=(4, 5))
    weights = exp_scores / totals[..., None, None]
    weights_low = weights.astype(jnp.bfloat16)
    dprobs = jnp.einsum(
        "ntkgd,neskd->nkgtes", grad_five, value_blocks, preferred_element_type=jnp.float32
    )
    deltas = jnp.sum(weights_low.astype(jnp.float32) * dprobs, axis=(4, 5))
    dscore = (weights * (dprobs - deltas[..., None, None]) * plain_row).astype(jnp.bfloat16)
    weights_row = weights_low * plain_row.astype(jnp.bfloat16)
    dquery = score_scale * jnp.einsum(
        "nkgtes,neskd->ntkgd", dscore, key_blocks, preferred_element_type=jnp.float32
    )
    key_term = score_scale * jnp.einsum(
        "nkgtes,ntkgd->neskd", dscore, query_five, preferred_element_type=jnp.float32
    )
    value_term = jnp.einsum(
        "nkgtes,ntkgd->neskd", weights_row, grad_five, preferred_element_type=jnp.float32
    )
    slot_terms = jnp.concatenate(
        [
            key_term.reshape(n_local * n_slots, BLK, kv_width),
            value_term.reshape(n_local * n_slots, BLK, kv_width),
        ],
        axis=2,
    )
    grad_buffer = (
        jnp.zeros((n_blocks, BLK, 2 * kv_width), jnp.float32)
        .at[slot_ids.reshape(-1)]
        .add(slot_terms)
    )
    local_index = global_id - first_block
    owns_row = (local_index >= 0) & (local_index < n_local)
    clipped = jnp.clip(local_index, 0, n_local - 1)
    row_query = lax.dynamic_slice_in_dim(query_now, clipped * BLK, BLK, 0)
    row_grad = lax.dynamic_slice_in_dim(upstream, clipped * BLK, BLK, 0)

    def whole_row(operands):
        head_query = operands[0].reshape(BLK, kv_heads, group_size, HD).transpose(1, 0, 2, 3)
        head_grad = operands[1].reshape(BLK, kv_heads, group_size, HD).transpose(1, 0, 2, 3)
        keys_heads = key_all.reshape(n_blocks * BLK, kv_heads, HD).transpose(1, 0, 2)
        values_heads = value_all.reshape(n_blocks * BLK, kv_heads, HD).transpose(1, 0, 2)

        def per_head(items):
            outputs = global_rows(
                items[0][None],
                items[1][None],
                items[2][None],
                items[3][None],
                score_scale,
                unchanged,
                unchanged,
            )
            return (outputs[0][0], outputs[1][0], outputs[2][0])

        row_dq, row_dk, row_dv = lax.map(
            per_head, (head_query, head_grad, keys_heads, values_heads)
        )
        row_dq = row_dq.transpose(1, 0, 2, 3).reshape(BLK, q_width)
        row_kv = jnp.concatenate(
            [
                row_dk.transpose(1, 0, 2).reshape(n_blocks * BLK, kv_width),
                row_dv.transpose(1, 0, 2).reshape(n_blocks * BLK, kv_width),
            ],
            axis=1,
        )
        return (row_dq, row_kv)

    def no_row(operands):
        return (
            jnp.zeros((BLK, q_width), jnp.float32),
            jnp.zeros((n_blocks * BLK, 2 * kv_width), jnp.float32),
        )

    row_dq, row_kv = lax.cond(owns_row, whole_row, no_row, (row_query, row_grad))
    grad_buffer = grad_buffer + row_kv.reshape(n_blocks, BLK, 2 * kv_width)
    query_flat = dquery.reshape(tok_rows, q_width)
    current_rows = lax.dynamic_slice_in_dim(query_flat, clipped * BLK, BLK, 0)
    query_flat = lax.dynamic_update_slice_in_dim(
        query_flat, current_rows + row_dq * owns_row.astype(jnp.float32), clipped * BLK, 0
    )
    flat_buffer = grad_buffer.reshape(n_blocks * BLK, 2 * kv_width)
    kv_summed = lax.psum_scatter(flat_buffer, "ctx", scatter_dimension=0, tiled=True)
    query_out = query_flat.astype(jnp.bfloat16)[None]
    key_out = kv_summed[:, :kv_width].astype(jnp.bfloat16)[None]
    value_out = kv_summed[:, kv_width:].astype(jnp.bfloat16)[None]
    return (query_out, key_out, value_out)


def solution(mesh):
    return jax.shard_map(
        per_device,
        mesh=mesh,
        in_specs=(
            P("segment", None, "ctx", None),
            P("segment", None, "ctx", None),
            P("segment", None, "ctx", None),
            P("segment", "ctx", None),
            P("segment"),
            P(),
        ),
        out_specs=(P("segment", "ctx", None), P("segment", "ctx", None), P("segment", "ctx", None)),
        check_vma=False,
    )
```

profile of v0, /device:TPU:0, one launch (start us, length us, event | category | flops | bytes accessed | tf_op | source)
XLA Modules:
  0.0 354.1 jit_solution(5291401676561156840)
XLA Ops:
  13.9 3.9 %collective-permute-start = (bf16[1,256,2048]{1,2,0:T(8,128)(2,1)}, bf16[1,256,2048]{1,2,0:T(8,128)(2,1)S(1)}, u32[]{:S(2)}, u32[]{:S(2)}) collective-permute-start(bf16[1,256,2048]{1,2,0:T(8,128)(2,1)} %copy.112), channel_id=1, source_target_pairs={{8,0},{16,8},{24,16},{0,24},{9,1},{17,9},{25,17},{1,25},{10,2},{18... | collective-permute-start | bytes 3145736 | tf_op jit(solution)/shard_map/ppermute | solution.py:13
  22.6 17.9 %collective-permute-done = bf16[1,256,2048]{1,2,0:T(8,128)(2,1)S(1)} collective-permute-done((bf16[1,256,2048]{1,2,0:T(8,128)(2,1)}, bf16[1,256,2048]{1,2,0:T(8,128)(2,1)S(1)}, u32[]{:S(2)}, u32[]{:S(2)}) %collective-permute-start) | collective-permute-done | bytes 1048608 | tf_op jit(solution)/shard_map/ppermute | solution.py:13
  47.4 4.3 %copy.106 = bf16[16,128,4,128]{3,1,2,0:T(8,128)(2,1)} copy(bf16[16,128,4,128]{1,0,3,2:T(8,128)(2,1)} %bitcast.257) | data formatting | bytes 4194304 | tf_op jit(solution)/shard_map/reshape | solution.py:83
  51.6 24.2 %all-gather.7.cloned.1.call-done = bf16[1,1,2048,512]{2,3,1,0:T(8,128)(2,1)} async-done(((bf16[1,1,256,512]{2,3,1,0:T(8,128)(2,1)}), bf16[1,1,2048,512]{2,3,1,0:T(8,128)(2,1)}) %all-gather.7.cloned.1.call-update) | async-done | bytes 2097168 | tf_op jit(solution)/shard_map/all_gather | solution.py:60
  79.4 4.3 %copy.111 = bf16[16,128,4,128]{3,1,2,0:T(8,128)(2,1)} copy(bf16[16,128,4,128]{1,0,3,2:T(8,128)(2,1)} %bitcast.258) | data formatting | bytes 4194304 | tf_op jit(solution)/shard_map/reshape | solution.py:84
  83.7 3.7 %gather_fusion = bf16[14,128,4,128]{3,1,2,0:T(8,128)(2,1)} fusion(bf16[16,128,4,128]{3,1,2,0:T(8,128)(2,1)} %copy.106, s32[1024]{0:T(1024)S(1)} %pad_clamp_fusion), kind=kCustom, calls=%fused_computation | custom fusion | bytes 3670072 | tf_op jit(solution)/shard_map/gather | solution.py:83
  87.4 3.7 %gather_fusion.1 = bf16[14,128,4,128]{3,1,2,0:T(8,128)(2,1)} fusion(bf16[16,128,4,128]{3,1,2,0:T(8,128)(2,1)} %copy.111, s32[1024]{0:T(1024)S(1)} %pad_clamp_fusion), kind=kCustom, calls=%fused_computation.1 | custom fusion | bytes 3670072 | tf_op jit(solution)/shard_map/gather | solution.py:84
  91.1 4.3 %bitcast_reduce_fusion.1 = (f32[2,4,4,128]{3,2,1,0:T(4,128)S(1)}, f32[2,4,7,128,128,4]{4,3,5,2,1,0:T(8,128)S(1)}) fusion(f32[2,7]{1,0:T(2,128)S(1)} %pad_maximum_fusion.2, bf16[2,128,4,4,128,1]{1,4,3,5,2,0:T(8,128)(2,1)S(1)} %copy.138, bf16[2,7,128,4,128,1]{4,2,3,1,0,5:T(8,128)(2,1)} %bitcast.255), kind=kOutput, calls=%fused_computation.55 | convolution fusion | flops 950530048 | bytes 17580088 | tf_op jit(solution)/shard_map/ntkgd,neskd->nkgtes/dot_general | solution.py:86
  95.4 7.6 %fusion.35 = (f32[2,4,4,128]{3,2,1,0:T(4,128)S(1)}, f32[2,4,7,128,128,4]{4,3,5,2,1,0:T(8,128)}) fusion(f32[2,4,4,128]{3,2,1,0:T(4,128)S(1)} %get-tuple-element.177, f32[2,7]{1,0:T(2,128)S(1)} %pad_maximum_fusion.2, f32[2,4,7,128,128,4]{4,3,5,2,1,0:T(8,128)S(1)} %get-tuple-element.178, bf16[2,128,4,4,128,1]{1,0,4,3,2,5:T(2,128)(2,1)S(1)} %bitcast.264, ...), kind=kOutput, calls=%fused_computation.50 | convolution fusion | flops 965210112 | bytes 32276536 | tf_op jit(solution)/shard_map/ntkgd,neskd->nkgtes/dot_general | solution.py:95
  104.9 10.4 %fusion.38 = bf16[2,4,4,128,7,128]{3,5,2,4,1,0:T(8,128)(2,1)} fusion(f32[2,4,7,128,128,4]{4,3,5,2,1,0:T(8,128)} %get-tuple-element.180, f32[2]{0:T(128)S(1)} %compare_convert_fusion, f32[2,4,4,128]{3,2,1,0:T(4,128)S(1)} %get-tuple-element.179, f32[2,4,4,128]{3,2,1,0:T(4,128)S(1)} %get-tuple-element.177, f32[2,7]{1,0:T(2,128)S(1)} %pad_maximum_fusion.2, ...), kind=kLoop, calls=%fused_computation.53 | loop fusion | flops 25690112 | bytes 36732992 | tf_op jit(solution)/shard_map/convert_element_type | solution.py:99
  115.4 5.4 %fusion.43 = f32[2,7,128,4,128]{2,4,1,3,0:T(8,128)S(1)} fusion(bf16[2,128,4,4,128,1]{1,4,3,5,2,0:T(8,128)(2,1)S(1)} %copy.138, bf16[2,4,4,128,7,128]{3,5,2,4,1,0:T(8,128)(2,1)} %fusion.38), kind=kOutput, calls=%fused_computation.63 | convolution fusion | flops 940441600 | bytes 12058624 | tf_op jit(solution)/shard_map/nkgtes,ntkgd->neskd/dot_general | solution.py:104
  122.9 9.0 %fusion.47 = f32[2,7,128,4,128]{2,4,1,3,0:T(8,128)} fusion(bf16[2]{0:T(256)(128)(2,1)S(1)} %fusion.65, bf16[2,128,4,4,128,1]{1,0,4,3,2,5:T(2,128)(2,1)S(1)} %bitcast.265, f32[2,4,7,128,128,4]{4,3,5,2,1,0:T(8,128)} %copy-done.2, f32[2,4,4,128]{3,2,1,0:T(4,128)S(1)} %get-tuple-element.177, f32[2,7]{1,0:T(2,128)S(1)} %pad_maximum_fusion.2), kind=kOutput, calls=%fused_computation.68 | convolution fusion | flops 957874176 | bytes 19415100 | tf_op jit(solution)/shard_map/nkgtes,ntkgd->neskd/dot_general | solution.py:107
  138.5 8.4 %copy.128 = f32[14,128,1024]{2,1,0:T(8,128)} copy(f32[14,128,1024]{1,2,0:T(8,128)} %pad_maximum_fusion.1) | data formatting | bytes 14680064 | tf_op jit(solution)/shard_map/concatenate | solution.py:110
  146.8 93.4 %conditional.1 = (f32[16,128,1024]{2,1,0:T(8,128)}, f32[128,2048]{1,0:T(8,128)S(1)}) conditional(s32[]{:T(128)} %convert_element_type.63, () %tuple.25, (s32[]{:T(128)}, s32[]{:T(128)}, bf16[1,8,256,2048]{3,2,1,0:T(8,128)(2,1)}, bf16[1,256,2048]{1,2,0:T(8,128)(2,1)S(1)}, bf16[2048,512]{0,1:T(8,128)(2,1)}, /*index=5*/bf16[2048,512]{0,1:T(8,128)(2,1)}) %tuple.26), branch_computations={%region_3.4_spmd, %region_4.9_spmd} | conditional | flops 1361378304 | bytes 111428864 | solution.py:165
  147.8 11.4 %copy.119 = bf16[1,8,256,2048]{2,3,1,0:T(8,128)(2,1)} copy(bf16[1,8,256,2048]{3,2,1,0:T(8,128)(2,1)} %get-tuple-element.150) | data formatting | bytes 16777216 | tf_op jit(solution)/shard_map
  162.1 42.7 %while.18 = (s32[]{:T(128)}, f32[4,128,4,128]{1,3,2,0:T(8,128)}, f32[4,2048,128]{2,1,0:T(8,128)}, f32[4,2048,128]{2,1,0:T(8,128)}, bf16[4,2048,128]{1,2,0:T(8,12...) while((s32[]{:T(128)}, f32[4,128,4,128]{1,3,2,0:T(8,128)}, ...), condition=%wide.region_8.8_spmd, body=%wide.region_5.7_spmd.sunk | while | flops 1359281152 | bytes 35931228 | solution.py:146
  204.9 7.3 %copy.99 = f32[2048,4,128]{2,1,0:T(4,128)} copy(f32[2048,4,128]{2,0,1:T(8,128)} %bitcast.260) | data formatting | bytes 8388608 | tf_op jit(solution)/shard_map/cond/branch_1_fun/transpose | solution.py:152
  212.1 5.5 %concatenate.38 = f32[16,128,512]{2,1,0:T(8,128)} reshape(f32[2048,4,128]{2,1,0:T(4,128)} %copy.99) | data formatting | bytes 8388608 | tf_op jit(solution)/shard_map/cond/branch_1_fun/concatenate | solution.py:150
  217.6 7.2 %copy.100 = f32[2048,4,128]{2,1,0:T(4,128)} copy(f32[2048,4,128]{2,0,1:T(8,128)} %bitcast.261) | data formatting | bytes 8388608 | tf_op jit(solution)/shard_map/cond/branch_1_fun/transpose | solution.py:153
  224.9 5.5 %concatenate.39 = f32[16,128,512]{2,1,0:T(8,128)} reshape(f32[2048,4,128]{2,1,0:T(4,128)} %copy.100) | data formatting | bytes 8388608 | tf_op jit(solution)/shard_map/cond/branch_1_fun/concatenate | solution.py:150
  230.3 8.2 %pad_maximum_fusion = f32[16,128,1024]{2,1,0:T(8,128)} fusion(f32[16,128,512]{2,1,0:T(8,128)} %concatenate.39, f32[16,128,512]{2,1,0:T(8,128)} %concatenate.38), kind=kLoop, calls=%fused_computation.45 | loop fusion | flops 2097152 | bytes 16777216 | tf_op jit(solution)/shard_map/cond/branch_1_fun/concatenate | solution.py:150
  240.3 17.5 %scatter_fusion = f32[16,128,1024]{2,1,0:T(8,128)} fusion(f32[16,128,1024]{2,1,0:T(8,128)} %get-tuple-element.111, s32[14]{0:T(128)S(1)} %copy-done.10, f32[14,128,1024]{2,1,0:T(8,128)} %copy.128), kind=kCustom, calls=%fused_computation.2 | custom fusion | flops 1835008 | bytes 22020152 | tf_op jit(solution)/shard_map/scatter-add | solution.py:120
  259.3 6.4 %fusion.46 = f32[2,128,4,4,128]{1,4,3,2,0:T(8,128)} fusion(bf16[2,4,4,128,7,128]{3,5,2,4,1,0:T(8,128)(2,1)} %fusion.38, bf16[2,7,128,4,128,1]{4,2,3,1,0,5:T(8,128)(2,1)S(1)} %bitcast.256), kind=kOutput, calls=%fused_computation.67 | convolution fusion | flops 940048384 | bytes 11272192 | tf_op jit(solution)/shard_map/nkgtes,neskd->ntkgd/dot_general | solution.py:101
  275.3 70.1 %reduce-scatter.2.cloned.1.call-done = f32[256,1024]{1,0:T(8,128)} async-done(((f32[2048,1024]{1,0:T(8,128)}), f32[256,1024]{1,0:T(8,128)}) %reduce-scatter.2.cloned.1.call-update) | async-done | bytes 1048592 | tf_op jit(solution)/shard_map/reduce_scatter | solution.py:173
  (105 shorter events, 93.0 us)
Async XLA Ops:
  7.2 1.6 copy-start
  7.2 10.6 %copy-start.9 = (s32[16,3]{0,1:T(4,128)S(1)}, s32[16,3]{0,1:T(4,128)}, u32[]{:S(2)}) copy-start(s32[16,3]{0,1:T(4,128)} %param.15) | copy-start | bytes 580
  7.2 36.6 %all-gather.5.cloned.1.call-start = ((), (), s32[]{:S(2)}) async-start(), calls=%async_computation.2 | async-start | bytes 2359296 | tf_op jit(solution)/shard_map/all_gather | solution.py:59
  9.7 66.2 %all-gather.7.cloned.1.call-start = ((), (), s32[]{:S(2)}) async-start(), calls=%async_computation.3 | async-start | bytes 2359296 | tf_op jit(solution)/shard_map/all_gather | solution.py:60
  11.6 333.9 %reduce-scatter.2.cloned.1.call-start = ((), (), s32[]{:S(2)}) async-start(), calls=%async_computation.1 | async-start | bytes 9437184 | tf_op jit(solution)/shard_map/reduce_scatter | solution.py:173
  13.9 26.6 %collective-permute-start = (bf16[1,256,2048]{1,2,0:T(8,128)(2,1)}, bf16[1,256,2048]{1,2,0:T(8,128)(2,1)S(1)}, u32[]{:S(2)}, u32[]{:S(2)}) collective-permute-start(bf16[1,256,2048]{1,2,0:T(8,128)(2,1)} %copy.112), channel_id=1, source_target_pairs={{8,0},{16,8},{24,16},{0,24},{9,1},{17,9},{25,17},{1,25},{10,2},{18... | collective-permute-start | bytes 3145736 | tf_op jit(solution)/shard_map/ppermute | solution.py:13
  91.1 4.3 %copy-start.8 = (bf16[14,128,4,128]{3,1,2,0:T(8,128)(2,1)S(1)}, bf16[14,128,4,128]{3,1,2,0:T(8,128)(2,1)}, u32[]{:S(2)}) copy-start(bf16[14,128,4,128]{3,1,2,0:T(8,128)(2,1)} %gather_fusion.1) | copy-start | bytes 5505028
  95.3 9.6 %copy-start.2 = (f32[2,4,7,128,128,4]{4,3,5,2,1,0:T(8,128)}, f32[2,4,7,128,128,4]{4,3,5,2,1,0:T(8,128)S(1)}, u32[]{:S(2)}) copy-start(f32[2,4,7,128,128,4]{4,3,5,2,1,0:T(8,128)S(1)} %get-tuple-element.178) | copy-start | bytes 44040196
  131.9 3.1 copy-start.3
  146.8 93.5 %copy-start.10 = (s32[14]{0:T(128)S(1)}, s32[14]{0:T(128)}, u32[]{:S(2)}) copy-start(s32[14]{0:T(128)} %fusion.64) | copy-start | bytes 172
  146.8 1.0 copy-start.7
  240.3 17.5 %copy-start.5 = (f32[128,2048]{1,0:T(8,128)}, f32[128,2048]{1,0:T(8,128)S(1)}, u32[]{:S(2)}) copy-start(f32[128,2048]{1,0:T(8,128)S(1)} %get-tuple-element.154) | copy-start | bytes 3145732
  257.8 1.5 copy-start.4
  265.6 4.4 %copy-start.6 = (f32[128,2048]{1,0:T(8,128)S(1)}, f32[128,2048]{1,0:T(8,128)}, u32[]{:S(2)}) copy-start(f32[128,2048]{1,0:T(8,128)} %copy-done.5) | copy-start | bytes 3145732
  270.0 77.5 %copy-start.1 = (bf16[1,8,256,512]{3,2,1,0:T(8,128)(2,1)S(1)}, bf16[1,8,256,512]{3,2,1,0:T(8,128)(2,1)}, u32[]{:S(2)}) copy-start(bf16[1,8,256,512]{3,2,1,0:T(8,128)(2,1)} %param.11) | copy-start | bytes 6291460
Sparse Core Ops, SparseCore 0:
  10.2 33.5 all-gather.4
  46.0 29.8 all-gather.6
  257.9 87.4 reduce-scatter.1
where the time goes:
time: 356 us; the launch traced here: 354 us
  waiting for transfers between devices  115 us (32%)
  local copies, waits for them, and re-layouts  97.6 us (27%)
  matrix products  71.6 us (20%)
  other arithmetic  50.6 us (14%)
  between operations  14.7 us (4%)
  starting transfers between devices  4.02 us (1%)
    reduce_scatter x1, waiting for transfers between devices, per_device(): lax.psum_scatter(flat_buffer, 'ctx', scatter_dimension=0, tiled=True)  70.1 us
    all_gather x1, waiting for transfers between devices, per_device(): lax.all_gather(value_now, 'ctx', axis=0, tiled=True)  24.2 us
    ppermute x1, waiting for transfers between devices, from_behind(): return lax.ppermute(block, axis, route)  17.9 us
    scatter-add x1, other arithmetic, per_device(): grad_buffer = jnp.zeros((n_blocks, BLK, 2 * kv_width), jnp.float32).at[sl...  17.5 us
    unnamed x25, local copies, waits for them, and re-layouts  16 us
    another operation x3, local copies, waits for them, and re-layouts  11.4 us
    concatenate x2, local copies, waits for them, and re-layouts, whole_row(): jnp.concatenate([row_dk.transpose(1, 0, 2).reshape(n_blocks * BLK, kv_wid...  10.9 us
    convert_element_type x1, other arithmetic, per_device(): (weights * (dprobs - deltas[..., None, None]) * plain_row).astype(jnp.bfl...  10.4 us
  transfers between devices with their start and end apart: 4, of which 4 were waited for; matrix products, arithmetic and copies ran while one was open for 9% of the time, Pallas kernels for 0%

commit v1 on v0

v1 whole, which is shorter than its diff:
```python
import functools

import jax
import jax.numpy as jnp
from jax import lax
from jax.experimental import pallas as pl
from jax.experimental.pallas import tpu as pltpu
from jax.sharding import PartitionSpec as P

HD = 128
BLK = 128
GROUP = 4
NSLOT = 7
LOG2E = 1.4426950408889634
MESH = pl.DeviceIdType.MESH


def dot(a, b, ca, cb):
    return lax.dot_general(a, b, (((ca,), (cb,)), ((), ())), preferred_element_type=jnp.float32)


def kernel(
    n_seg, nz, rb_ref, q_in, g_in, kv_in, dq_out, kv_out,
    q0, q1, g0, g1, kv0, kv1, slk0, slk1, slv0, slv1,
    rr0, rr1, rl0, rl1, dq0, dq1, fin0, fin1,
    kgat, vgat, dsb, pbb, tab,
    swap_s, swap_r, grad_s, grad_r, ga_s, ga_r, rs_s, rs_r, out_s, out_r,
):
    seg = lax.axis_index("segment")
    ctx = lax.axis_index("ctx")
    z = ctx // 2
    core = ctx % 2
    other = 1 - core
    nb = nz * 4
    q_sc, g_sc, kv_sc = (q0, q1), (g0, g1), (kv0, kv1)
    slk, slv = (slk0, slk1), (slv0, slv1)
    rs_buf = ((rr0, rl0), (rr1, rl1))
    dq_sc, fin = (dq0, dq1), (fin0, fin1)
    scale = HD ** (-0.5)
    partner = (seg, ctx + 1 - 2 * core)
    right = (seg, ctx + 2)
    left = (seg, ctx - 2)
    ahead = lax.rem(seg + 1, n_seg)
    behind = lax.rem(seg + n_seg - 1, n_seg)
    has_left, has_right = z > 0, z < nz - 1

    def rcopy(src, dst, ss, rs, dev):
        return pltpu.make_async_remote_copy(
            src_ref=src, dst_ref=dst, send_sem=ss, recv_sem=rs, device_id=dev, device_id_type=MESH
        )

    barrier = pltpu.get_barrier_semaphore()
    for dev in (
        partner, (ahead, z * 2), (ahead, z * 2 + 1), (behind, z * 2), (behind, z * 2 + 1)
    ):
        pl.semaphore_signal(barrier, inc=1, device_id=dev, device_id_type=MESH)

    @pl.when(has_left)
    def _():
        pl.semaphore_signal(barrier, inc=1, device_id=left, device_id_type=MESH)

    @pl.when(has_right)
    def _():
        pl.semaphore_signal(barrier, inc=1, device_id=right, device_id_type=MESH)

    pl.semaphore_wait(barrier, 5 + has_left.astype(jnp.int32) + has_right.astype(jnp.int32))

    def swap_kv(h):
        return rcopy(
            kv_in.at[other * 2 + h], kv_sc[h].at[pl.ds(z * 8 + core * 4, 4)],
            swap_s.at[0, h], swap_r.at[0, h], partner,
        )

    def swap_q(h):
        return rcopy(
            q_in.at[other * 2 + h], q_sc[h].at[pl.ds(core * 2, 2)],
            swap_s.at[1, h], swap_r.at[1, h], partner,
        )

    def hand_off(h, c):
        return rcopy(
            g_in.at[c * 2 + h], g_sc[h].at[pl.ds(core * 2, 2)],
            grad_s.at[h, c], grad_r.at[h, core], (behind, z * 2 + c),
        )

    def hand_off_in(h, c):
        part = g_sc[h].at[pl.ds(c * 2, 2)]
        return rcopy(part, part, grad_s.at[h, c], grad_r.at[h, c], (ahead, z * 2 + c))

    def chunk_copy(h, d, j):
        part = kv_sc[h].at[pl.ds(j * 8, 8)]
        return rcopy(part, part, ga_s.at[h, d, j], ga_r.at[h, j], left if d else right)

    def send_own(h):
        @pl.when(has_right)
        def _():
            chunk_copy(h, 0, z).start()

        @pl.when(has_left)
        def _():
            chunk_copy(h, 1, z).start()

    def hop(h, dist):
        @pl.when(z >= dist)
        def _():
            chunk_copy(h, 0, z - dist).wait_recv()

            @pl.when(has_right)
            def _():
                chunk_copy(h, 0, z - dist).start()

        @pl.when(z + dist <= nz - 1)
        def _():
            chunk_copy(h, 1, z + dist).wait_recv()

            @pl.when(has_left)
            def _():
                chunk_copy(h, 1, z + dist).start()

    def hop_sends(h):
        for dist in range(nz):
            @pl.when((z >= dist) & has_right)
            def _():
                chunk_copy(h, 0, z - dist).wait_send()

            @pl.when((z + dist <= nz - 1) & has_left)
            def _():
                chunk_copy(h, 1, z + dist).wait_send()

    for h in range(2):
        swap_kv(h).start()
    for h in range(2):
        for c in range(2):
            hand_off(h, c).start()
        swap_q(h).start()

    for h in range(2):
        kv_sc[h][pl.ds(z * 8 + core * 4, 4)] = kv_in[core * 2 + h]
        q_sc[h][pl.ds(core * 2, 2)] = q_in[core * 2 + h]

    swap_kv(0).wait_recv()
    send_own(0)

    for h in range(2):
        slk[h][NSLOT] = jnp.zeros((BLK, HD), jnp.float32)
        slv[h][NSLOT] = jnp.zeros((BLK, HD), jnp.float32)

    def slots(r):
        b = z * 4 + r
        ids = [lax.rem(b + nb - 1, nb), b, lax.rem(b + 1, nb), 0]
        ids += [rb_ref[b * 3 + i] for i in range(3)]
        extra = (b != 0) & (b != 1) & (b != nb - 1)
        return b, ids, extra

    def fill(c, _):
        for r in range(4):
            b, ids, extra = slots(r)
            where = jnp.where(extra & (c == 0), r * 8 + 3, NSLOT)
            for s in (0, 1, 2, 4, 5, 6):
                where = jnp.where(ids[s] == c, r * 8 + s, where)
            tab[r * nb + c] = jnp.where(b == 0, 32 + c, where)
        return 0

    lax.fori_loop(0, nb, fill, 0)

    def attend(h, r, n, base, extra):
        width = n * BLK
        if extra is not None:
            lane = lax.broadcasted_iota(jnp.int32, (1, width), 1) // BLK
            keep = jnp.where(lane == 3, extra.astype(jnp.float32), 1.0)

        def head(g):
            query, grad = q_sc[h][r, g], g_sc[h][r, g]
            exp_s = jnp.exp2(dot(query, kgat[:width], 1, 1) * (scale * LOG2E))
            if extra is not None:
                exp_s = exp_s * keep
            total = jnp.sum(exp_s, axis=1, keepdims=True)
            shrink = jnp.where(total > 1.0, 2.0**-8, 1.0)
            p = (exp_s * shrink) * (1.0 / (total * shrink))
            p_low = p.astype(jnp.bfloat16)
            dp = dot(grad, vgat[:width], 1, 1)
            delta = jnp.sum(p_low.astype(jnp.float32) * dp, axis=1, keepdims=True)
            ds = (p * (dp - delta)).astype(jnp.bfloat16)
            rows = pl.ds(pl.multiple_of(g * BLK, BLK), BLK)
            pbb[rows, :width] = p_low
            dsb[rows, :width] = ds
            dq = dot(ds, kgat[:width], 1, 0) * scale
            dq_sc[h][r, g] = dq.astype(jnp.bfloat16)

        if extra is None:
            @pl.loop(0, GROUP)
            def _(g):
                head(g)
        else:
            for g in range(GROUP):
                head(g)
        q_t = q_sc[h][r].reshape(GROUP * BLK, HD).T
        g_t = g_sc[h][r].reshape(GROUP * BLK, HD).T
        dk = dot(q_t, dsb[:, :width], 1, 0)
        for s in range(n):
            slk[h][base + s] = dk[:, s * BLK:(s + 1) * BLK]
        dv = dot(g_t, pbb[:, :width], 1, 0)
        for s in range(n):
            slv[h][base + s] = dv[:, s * BLK:(s + 1) * BLK]

    def row(h, r):
        b, ids, extra = slots(r)

        @pl.when(b == 0)
        def _():
            for c in range(nb):
                tile = (c // 2) * 4 + c % 2
                kgat[c * BLK:(c + 1) * BLK] = kv_sc[h][tile]
                vgat[c * BLK:(c + 1) * BLK] = kv_sc[h][tile + 2]
            attend(h, r, nb, 32, None)

        @pl.when(b != 0)
        def _():
            for s in range(NSLOT):
                tile = (ids[s] >> 1) * 4 + (ids[s] & 1)
                kgat[s * BLK:(s + 1) * BLK] = kv_sc[h][tile]
                vgat[s * BLK:(s + 1) * BLK] = kv_sc[h][tile + 2]
            attend(h, r, NSLOT, r * 8, extra)

    def rows(h, first, last):
        @pl.loop(first, last)
        def _(r):
            row(h, r)

    def terms(h, j, m):
        c = j * 4 + m
        at = [tab[r * nb + c] for r in range(4)]
        dk = (slk[h][at[0]] + slk[h][at[1]]) + (slk[h][at[2]] + slk[h][at[3]])
        dv = (slv[h][at[0]] + slv[h][at[1]]) + (slv[h][at[2]] + slv[h][at[3]])
        return dk, dv

    def sum_copy(h, d, j):
        part = rs_buf[h][d].at[pl.ds(j * 8, 8)]
        return rcopy(part, part, rs_s.at[h, d, j], rs_r.at[h, d, j], left if d else right)

    def add_own(h, d, j, first):
        buf = rs_buf[h][d]

        @pl.loop(0, 4)
        def _(m):
            dk, dv = terms(h, j, m)
            k = j * 8 + (m // 2) * 4 + m % 2
            if not first:
                dk = dk + buf[k].astype(jnp.float32)
                dv = dv + buf[k + 2].astype(jnp.float32)
            buf[k] = dk.astype(jnp.bfloat16)
            buf[k + 2] = dv.astype(jnp.bfloat16)

    def sum_step(h, t):
        for d in range(2):
            i = nz - 1 - z if d else z
            to = i + nz - 1 - t
            j = nz - 1 - to if d else to

            @pl.when(i == 0)
            def _():
                add_own(h, d, j, True)
                sum_copy(h, d, j).start()

            if t:
                @pl.when((i > 0) & (i <= t))
                def _():
                    sum_copy(h, d, j).wait_recv()
                    add_own(h, d, j, False)
                    sum_copy(h, d, j).start()

    def sum_sends(h):
        for t in range(nz - 1):
            for d in range(2):
                i = nz - 1 - z if d else z
                to = i + nz - 1 - t
                j = nz - 1 - to if d else to

                @pl.when(i <= t)
                def _():
                    sum_copy(h, d, j).wait_send()

    def kv_back(h):
        return rcopy(
            fin[h].at[other], kv_out.at[core * 2 + h], out_s.at[0, h], out_r.at[0, h], partner
        )

    def dq_back(h):
        return rcopy(
            dq_sc[h].at[pl.ds(other * 2, 2)], dq_out.at[core * 2 + h],
            out_s.at[1, h], out_r.at[1, h], partner,
        )

    def finish(h):
        @pl.when(has_left)
        def _():
            sum_copy(h, 0, z).wait_recv()

        @pl.when(has_right)
        def _():
            sum_copy(h, 1, z).wait_recv()

        from_left = has_left.astype(jnp.float32)
        from_right = has_right.astype(jnp.float32)

        @pl.loop(0, 4)
        def _(m):
            dk, dv = terms(h, z, m)
            k = (m // 2) * 4 + m % 2
            parts = []
            for total, e in ((dk, 0), (dv, 2)):
                at_left = rs_buf[h][0][z * 8 + k + e].astype(jnp.float32)
                at_right = rs_buf[h][1][z * 8 + k + e].astype(jnp.float32)
                total = total + jnp.where(from_left > 0, at_left, 0.0)
                parts.append(total + jnp.where(from_right > 0, at_right, 0.0))
            fin[h][m // 2, m % 2] = (parts[0].T * scale).astype(jnp.bfloat16)
            fin[h][m // 2, m % 2 + 2] = parts[1].T.astype(jnp.bfloat16)

        kv_back(h).start()
        kv_out[core * 2 + h] = fin[h][core]

    for dist in range(1, nz):
        hop(0, dist)
        if dist == max(nz - 2, 1):
            swap_kv(1).wait_recv()
            send_own(1)
    hop(1, 1)
    for h in range(2):
        swap_q(h).wait_recv()
    for c in range(2):
        hand_off_in(0, c).wait_recv()
    rows(0, 0, 2)
    for dist in range(2, nz - 1):
        hop(1, dist)
    rows(0, 2, 4)
    if nz > 2:
        hop(1, nz - 1)
    for c in range(2):
        hand_off_in(1, c).wait_recv()
    sum_step(0, 0)
    dq_back(0).start()
    rows(1, 0, 2)
    for t in range(1, nz - 2):
        sum_step(0, t)
    rows(1, 2, 4)
    if nz > 2:
        sum_step(0, nz - 2)
    sum_step(1, 0)
    dq_back(1).start()
    for h in range(2):
        dq_out[core * 2 + h] = dq_sc[h][pl.ds(core * 2, 2)]
    finish(0)
    for t in range(1, nz - 1):
        sum_step(1, t)
    finish(1)

    for h in range(2):
        swap_kv(h).wait_send()
        swap_q(h).wait_send()
        for c in range(2):
            hand_off(h, c).wait_send()
        hop_sends(h)
        sum_sends(h)
        dq_back(h).wait()
        kv_back(h).wait()


def per_device(n_seg, n_ctx, queries, keys, values, grad_slab, plan, random_blocks):
    nz = n_ctx // 2
    nb = nz * 4
    mb = plan[0]
    query_now = lax.dynamic_index_in_dim(queries[0], mb, 0, keepdims=False)
    key_now = lax.dynamic_index_in_dim(keys[0], mb, 0, keepdims=False)
    value_now = lax.dynamic_index_in_dim(values[0], mb, 0, keepdims=False)
    q_in = query_now.reshape(2, BLK, 4, GROUP, HD).transpose(2, 0, 3, 1, 4)
    g_in = grad_slab[0].reshape(2, BLK, 4, GROUP, HD).transpose(2, 0, 3, 1, 4)
    kv_in = jnp.concatenate(
        [
            key_now.reshape(2, BLK, 4, HD).transpose(2, 0, 1, 3),
            value_now.reshape(2, BLK, 4, HD).transpose(2, 0, 1, 3),
        ],
        axis=1,
    )
    low = jnp.bfloat16
    vmem = pl.BlockSpec(memory_space=pltpu.VMEM)
    dma = pltpu.SemaphoreType.DMA
    rows4 = pltpu.VMEM((4, GROUP, BLK, HD), low)
    line = pltpu.VMEM((nb * 2, BLK, HD), low)
    tiles = pltpu.VMEM((32 + nb, BLK, HD), jnp.float32)
    dq, dkv = pl.pallas_call(
        functools.partial(kernel, n_seg, nz),
        out_shape=(
            jax.ShapeDtypeStruct((4, 2, GROUP, BLK, HD), low),
            jax.ShapeDtypeStruct((4, 4, BLK, HD), low),
        ),
        in_specs=[pl.BlockSpec(memory_space=pltpu.SMEM), vmem, vmem, vmem],
        out_specs=(vmem, vmem),
        scratch_shapes=[
            rows4, rows4, rows4, rows4, line, line, tiles, tiles, tiles, tiles,
            line, line, line, line, rows4, rows4,
            pltpu.VMEM((2, 4, BLK, HD), low), pltpu.VMEM((2, 4, BLK, HD), low),
            pltpu.VMEM((nb * BLK, HD), low), pltpu.VMEM((nb * BLK, HD), low),
            pltpu.VMEM((GROUP * BLK, nb * BLK), low), pltpu.VMEM((GROUP * BLK, nb * BLK), low),
            pltpu.SMEM((4 * nb,), jnp.int32),
            dma((2, 2)), dma((2, 2)), dma((2, 2)), dma((2, 2)),
            dma((2, 2, nz)), dma((2, nz)), dma((2, 2, nz)), dma((2, 2, nz)),
            dma((2, 2)), dma((2, 2)),
        ],
        compiler_params=pltpu.CompilerParams(
            collective_id=0, has_side_effects=True, vmem_limit_bytes=60 * 1024 * 1024
        ),
        cost_estimate=pl.CostEstimate(
            flops=6_000_000_000, bytes_accessed=8_000_000, transcendentals=6_000_000
        ),
    )(random_blocks.reshape(-1), q_in, g_in, kv_in)
    query_grad = dq.transpose(1, 3, 0, 2, 4).reshape(1, 2 * BLK, -1)
    key_grad = dkv[:, :2].transpose(1, 2, 0, 3).reshape(1, 2 * BLK, -1)
    value_grad = dkv[:, 2:].transpose(1, 2, 0, 3).reshape(1, 2 * BLK, -1)
    return (query_grad, key_grad, value_grad)


def solution(mesh):
    return jax.shard_map(
        functools.partial(per_device, mesh.shape["segment"], mesh.shape["ctx"]),
        mesh=mesh,
        in_specs=(
            P("segment", None, "ctx", None),
            P("segment", None, "ctx", None),
            P("segment", None, "ctx", None),
            P("segment", "ctx", None),
            P("segment"),
            P(),
        ),
        out_specs=(P("segment", "ctx", None), P("segment", "ctx", None), P("segment", "ctx", None)),
        check_vma=False,
    )
```

time: 356 us -> 108 us (0.30)
  waiting for transfers between devices: 115 us -> 0 us
  Pallas kernels: 0 us -> 90.7 us
  local copies, waits for them, and re-layouts: 97.6 us -> 14.2 us
  matrix products: 71.6 us -> 0 us
  other arithmetic: 50.6 us -> 0.84 us
  between operations: 14.7 us -> 1.37 us
  starting transfers between devices: 4.02 us -> 0 us
    pallas_call x0 -> x1, Pallas kernels: none -> 90.7 us  [per_device(): pl.pallas_call(functools.partial(kernel, n_seg, nz), out_shape=(jax.Shape...]
    dot_general x25 -> x0, matrix products: 71.6 us -> none  [the longest x1 9 us: per_device(): jnp.einsum('nkgtes,ntkgd->neskd', weights_row, grad_five, preferred_eleme...]
    reduce_scatter x1 -> x0, waiting for transfers between devices: 70.1 us -> none  [per_device(): lax.psum_scatter(flat_buffer, 'ctx', scatter_dimension=0, tiled=True)]
    all_gather x2 -> x0, waiting for transfers between devices: 27.2 us -> none  [the longest x1 24.2 us: per_device(): lax.all_gather(value_now, 'ctx', axis=0, tiled=True)]
    concatenate x10 -> x0, local copies, waits for them, and re-layouts: 19.8 us -> none  [the longest x2 10.9 us: whole_row(): jnp.concatenate([row_dk.transpose(1, 0, 2).reshape(n_blocks * BLK, kv_wid...]
    ppermute x1 -> x0, waiting for transfers between devices: 17.9 us -> none  [from_behind(): return lax.ppermute(block, axis, route)]
    scatter-add x1 -> x0, other arithmetic: 17.5 us -> none  [per_device(): grad_buffer = jnp.zeros((n_blocks, BLK, 2 * kv_width), jnp.float32).at[sl...]
    unnamed x25 -> x3, local copies, waits for them, and re-layouts: 16 us -> 0.76 us
  transfers between devices with their start and end apart: 4 -> 0, of which waited for: 4 -> 0; matrix products, arithmetic and copies ran while one was open for 9% -> 0% of each run, Pallas kernels for 0% -> 0%
where the time goes in v1:
time: 108 us; the launch traced here: 107 us
  Pallas kernels  90.7 us (84%)
  local copies, waits for them, and re-layouts  14.2 us (13%)
  between operations  1.37 us (1%)
    pallas_call x1, Pallas kernels, per_device(): pl.pallas_call(functools.partial(kernel, n_seg, nz), out_shape=(jax.Shape...  90.7 us

profile of v1, /device:TPU:0, one launch (start us, length us, event | category | flops | bytes accessed | tf_op | source)
XLA Modules:
  0.0 107.1 jit_solution(12034969589523373925)
XLA Ops:
  0.6 0.8 copy.10
  1.4 0.6 reshape.36.rb_ref
  2.0 1.8 %reshape_squeeze.3 = bf16[2,128,4,4,128]{4,3,2,1,0:T(4,128)(2,1)S(1)} reshape(bf16[1,256,2048]{2,1,0:T(8,128)(2,1)} %param.9) | data formatting | bytes 2097152 | tf_op jit(solution)/shard_map/reshape;squeeze | solution.py:376
  4.4 1.3 %constant_dynamic-slice_fusion.2 = bf16[1,1,256,2048]{3,2,1,0:T(8,128)(2,1)S(1)} fusion(bf16[1,8,256,2048]{3,2,1,0:T(8,128)(2,1)} %param.6, s32[]{:T(128)S(6)} %select_n.7), kind=kLoop, calls=%fused_computation.9 | loop fusion | bytes 2097156 | tf_op jit(solution)/shard_map/jit(dynamic_index_in_dim)/dynamic_slice | solution.py:372
  5.7 0.8 reshape.37
  6.5 1.9 %copy_bitcast_fusion = (bf16[4,2,4,128,128]{4,3,2,1,0:T(8,128)(2,1)}, bf16[4,2,4,128,128]{4,3,2,1,0:T(8,128)(2,1)}) fusion(bf16[2,128,4,4,128]{4,3,2,1,0:T(4,128)(2,1)S(1)} %reshape_squeeze.3, bf16[2,128,4,4,128]{4,3,2,1,0:T(4,128)(2,1)S(1)} %reshape.37), kind=kLoop, calls=%fused_computation | loop fusion | bytes 4194304 | tf_op jit(solution)/shard_map/transpose | solution.py:376
  8.4 1.1 constant_dynamic-slice_fusion
  9.5 0.1 reshape.39
  9.6 0.1 reshape.38
  9.7 0.8 pad_maximum_fusion.kv_in
  10.6 90.7 %shard_map.85 = (bf16[4,2,4,128,128]{4,3,2,1,0:T(8,128)(2,1)}, bf16[4,4,128,128]{3,2,1,0:T(8,128)(2,1)}) custom-call(s32[48]{0:T(128)} %reshape.36.rb_ref, bf16[4,2,4,128,128]{4,3,2,1,0:T(8,128)(2,1)} %get-tuple-element.12.q_in, bf16[4,2,4,128,128]{4,3,2,1,0:T(8,128)(2,1)} %get-tuple-element.11.g_in, bf16[4,4,128,128]{3,2,1,0:T(8,128)(2,1)} %pad_maximum_fusion.kv_in), custom_call_target="tpu_custom_call" | custom-call | flops 6000000000 | bytes 8000000 | tf_op jit(solution)/shard_map/pallas_call | solution.py:390
  101.3 0.0 copy-start
  101.3 2.1 %copy.15 = bf16[2,128,4,4,128]{4,3,2,1,0:T(4,128)(2,1)S(1)} copy(bf16[2,128,4,4,128]{4,1,3,0,2:T(8,128)(2,1)} %bitcast.25) | data formatting | bytes 2097152 | tf_op jit(solution)/shard_map/transpose | solution.py:416
  103.4 1.6 %reshape.40 = bf16[1,256,2048]{2,1,0:T(8,128)(2,1)} reshape(bf16[2,128,4,4,128]{4,3,2,1,0:T(4,128)(2,1)S(1)} %copy.15) | data formatting | bytes 2097152 | tf_op jit(solution)/shard_map/reshape | solution.py:416
  105.0 0.0 copy-done
  105.0 0.2 copy.16
  105.2 0.8 reshape.41
  106.0 0.2 copy.17
  106.3 0.8 reshape.42
  (3 shorter events, 0.1 us)
Async XLA Ops:
  101.3 3.7 %copy-start = (bf16[4,4,128,128]{3,2,1,0:T(8,128)(2,1)S(1)}, bf16[4,4,128,128]{3,2,1,0:T(8,128)(2,1)}, u32[]{:S(2)}) copy-start(bf16[4,4,128,128]{3,2,1,0:T(8,128)(2,1)} %get-tuple-element.6) | copy-start | bytes 1572868

commit v2 on v1

v2 whole, which is shorter than its diff:
```python
import functools

import jax
import jax.numpy as jnp
from jax import lax
from jax.experimental import pallas as pl
from jax.experimental.pallas import tpu as pltpu
from jax.sharding import PartitionSpec as P

HD = 128
BLK = 128
GROUP = 4
NSLOT = 7
LOG2E = 1.4426950408889634
MESH = pl.DeviceIdType.MESH


def dot(a, b, ca, cb):
    return lax.dot_general(a, b, (((ca,), (cb,)), ((), ())), preferred_element_type=jnp.float32)


def kernel(
    n_seg, nz, rb_ref, q_in, g_in, k_in, v_in, dq_out, dk_out, dv_out,
    q_sc, g_sc, dq_sc, k0, v0, k1, v1, slv0, slk0, slv1, slk1, sums, fin,
    kgat, vgat, s_ref, dsb, p_plain, p_full, tab,
    swap_s, swap_r, qs_s, qs_r, grad_s, grad_r, ga_s, ga_r, rs_s, rs_r,
    dq_s, dq_r, out_s, out_r,
):
    seg = lax.axis_index("segment")
    ctx = lax.axis_index("ctx")
    z = ctx // 2
    core = ctx % 2
    other = 1 - core
    nb = nz * 4
    line = (k0, v0, k1, v1)
    terms_of = (slv0, slk0, slv1, slk1)
    scale = HD ** (-0.5)
    partner = (seg, ctx + 1 - 2 * core)
    right = (seg, ctx + 2)
    left = (seg, ctx - 2)
    ahead = lax.rem(seg + 1, n_seg)
    behind = lax.rem(seg + n_seg - 1, n_seg)
    has_left, has_right = z > 0, z < nz - 1

    def rcopy(src, dst, ss, rs, dev):
        return pltpu.make_async_remote_copy(
            src_ref=src, dst_ref=dst, send_sem=ss, recv_sem=rs, device_id=dev, device_id_type=MESH
        )

    def cols(at):
        return pl.ds(pl.multiple_of(at * HD, HD), HD)

    def block(b):
        return pl.ds(b * BLK, BLK)

    barrier = pltpu.get_barrier_semaphore()
    for dev in (
        partner, (ahead, z * 2), (ahead, z * 2 + 1), (behind, z * 2), (behind, z * 2 + 1)
    ):
        pl.semaphore_signal(barrier, inc=1, device_id=dev, device_id_type=MESH)

    @pl.when(has_left)
    def _():
        pl.semaphore_signal(barrier, inc=1, device_id=left, device_id_type=MESH)

    @pl.when(has_right)
    def _():
        pl.semaphore_signal(barrier, inc=1, device_id=right, device_id_type=MESH)

    pl.semaphore_wait(barrier, 5 + has_left.astype(jnp.int32) + has_right.astype(jnp.int32))

    def swap_kv(u):
        source = v_in if u % 2 else k_in
        for b in range(2):
            rcopy(
                source.at[block(b), cols(other * 2 + u // 2)], line[u].at[z * 4 + core * 2 + b],
                swap_s.at[u], swap_r.at[u], partner,
            ).start()

    def swap_kv_all(u):
        part = line[u].at[pl.ds(z * 4 + other * 2, 2)]
        return rcopy(part, part, swap_s.at[u], swap_r.at[u], partner)

    def swap_q(h):
        for b in range(2):
            for g in range(GROUP):
                rcopy(
                    q_in.at[block(b), cols((other * 2 + h) * GROUP + g)],
                    q_sc.at[h, core * 2 + b, g], qs_s.at[h], qs_r.at[h], partner,
                ).start()

    def swap_q_all(h):
        part = q_sc.at[h, pl.ds(other * 2, 2)]
        return rcopy(part, part, qs_s.at[h], qs_r.at[h], partner)

    def hand_off(h):
        for c in range(2):
            for b in range(2):
                for g in range(GROUP):
                    rcopy(
                        g_in.at[0, block(b), cols((c * 2 + h) * GROUP + g)],
                        g_sc.at[h, core * 2 + b, g],
                        grad_s.at[h, c], grad_r.at[h, core], (behind, z * 2 + c),
                    ).start()

    def hand_off_all(h, c):
        part = g_sc.at[h, pl.ds(c * 2, 2)]
        return rcopy(part, part, grad_s.at[h, c], grad_r.at[h, c], (ahead, z * 2 + c))

    def chunk_copy(u, d, j):
        part = line[u].at[pl.ds(j * 4, 4)]
        return rcopy(part, part, ga_s.at[u, d, j], ga_r.at[u, j], left if d else right)

    def send_own(u):
        swap_kv_all(u).wait_recv()

        @pl.when(has_right)
        def _():
            chunk_copy(u, 0, z).start()

        @pl.when(has_left)
        def _():
            chunk_copy(u, 1, z).start()

    def hop(u, dist):
        @pl.when(z >= dist)
        def _():
            chunk_copy(u, 0, z - dist).wait_recv()

            @pl.when(has_right)
            def _():
                chunk_copy(u, 0, z - dist).start()

        @pl.when(z + dist <= nz - 1)
        def _():
            chunk_copy(u, 1, z + dist).wait_recv()

            @pl.when(has_left)
            def _():
                chunk_copy(u, 1, z + dist).start()

    def hop_sends(u):
        for dist in range(nz):
            @pl.when((z >= dist) & has_right)
            def _():
                chunk_copy(u, 0, z - dist).wait_send()

            @pl.when((z + dist <= nz - 1) & has_left)
            def _():
                chunk_copy(u, 1, z + dist).wait_send()

    swap_kv(0)
    hand_off(0)
    swap_q(0)
    for u in range(4):
        source = v_in if u % 2 else k_in
        if u:
            swap_kv(u)
        for b in range(2):
            line[u][z * 4 + core * 2 + b] = source[block(b), cols(core * 2 + u // 2)]
        if u == 0:
            send_own(0)
    swap_q(1)
    for h in range(2):
        for b in range(2):
            for g in range(GROUP):
                q_sc[h, core * 2 + b, g] = q_in[block(b), cols((core * 2 + h) * GROUP + g)]

    for u in range(4):
        terms_of[u][NSLOT] = jnp.zeros((BLK, HD), jnp.float32)

    def slots(r):
        b = z * 4 + r
        ids = [lax.rem(b + nb - 1, nb), b, lax.rem(b + 1, nb), 0]
        ids += [rb_ref[b, i] for i in range(3)]
        extra = (b != 0) & (b != 1) & (b != nb - 1)
        return b, ids, extra

    def fill(c, _):
        for r in range(4):
            b, ids, extra = slots(r)
            where = jnp.where(extra & (c == 0), r * 8 + 3, NSLOT)
            for s in (0, 1, 2, 4, 5, 6):
                where = jnp.where(ids[s] == c, r * 8 + s, where)
            tab[r * nb + c] = jnp.where(b == 0, 32 + c, where)
        return 0

    lax.fori_loop(0, nb, fill, 0)

    def chunk_loop(n, step):
        size = 64
        while size * n > 512 and size > 16:
            size //= 2

        def run(i, _):
            step(pl.ds(pl.multiple_of(i * size, size), size))
            return 0

        lax.fori_loop(0, GROUP * BLK // size, run, 0, unroll=2)

    def lanes(t):
        return slice(t * BLK, (t + 1) * BLK)

    def total_of(tiles):
        tiles = list(tiles)
        while len(tiles) > 1:
            pairs = [a + b for a, b in zip(tiles[::2], tiles[1::2])]
            tiles = pairs + tiles[len(pairs) * 2:]
        return jnp.sum(tiles[0], axis=1, keepdims=True)

    def probs(h, r, n, base, extra, p_ref):
        width = n * BLK
        s_ref[:, :width] = dot(q_sc[h, r].reshape(GROUP * BLK, HD), kgat[:width], 1, 1)
        keep = None if extra is None else extra.astype(jnp.float32)

        def step(at):
            exp_s = [jnp.exp2(s_ref[at, lanes(t)] * (scale * LOG2E)) for t in range(n)]
            if keep is not None:
                exp_s[3] = exp_s[3] * keep
            total = total_of(exp_s)
            shrink = jnp.where(total > 1.0, 2.0**-8, 1.0)
            inverse = 1.0 / (total * shrink)
            for t in range(n):
                p_ref[at, lanes(t)] = ((exp_s[t] * shrink) * inverse).astype(jnp.bfloat16)

        chunk_loop(n, step)
        dv = dot(g_sc[h, r].reshape(GROUP * BLK, HD).T, p_ref[:, :width], 1, 0)
        for t in range(n):
            terms_of[2 * h][base + t] = dv[:, lanes(t)]

    def grads(h, r, n, base, p_ref):
        width = n * BLK
        s_ref[:, :width] = dot(g_sc[h, r].reshape(GROUP * BLK, HD), vgat[:width], 1, 1)

        def step(at):
            dp = [s_ref[at, lanes(t)] for t in range(n)]
            p = [p_ref[at, lanes(t)].astype(jnp.float32) for t in range(n)]
            delta = total_of([a * b for a, b in zip(p, dp)])
            for t in range(n):
                dsb[at, lanes(t)] = (p[t] * (dp[t] - delta)).astype(jnp.bfloat16)

        chunk_loop(n, step)
        dq = dot(dsb[:, :width], kgat[:width], 1, 0) * scale
        dq_sc[h, r] = dq.astype(jnp.bfloat16).reshape(GROUP, BLK, HD)
        dk = dot(q_sc[h, r].reshape(GROUP * BLK, HD).T, dsb[:, :width], 1, 0)
        for t in range(n):
            terms_of[2 * h + 1][base + t] = dk[:, lanes(t)]

    def rows(phase, h, first, last):
        keys, values = line[2 * h], line[2 * h + 1]

        def pick(ids):
            for s, c in enumerate(ids):
                kgat[lanes(s)] = keys[c]
                if phase:
                    vgat[lanes(s)] = values[c]

        @pl.loop(first, last)
        def _(r):
            b, ids, extra = slots(r)

            @pl.when(b == 0)
            def _():
                pick(range(nb))
                if phase:
                    grads(h, r, nb, 32, p_full)
                else:
                    probs(h, r, nb, 32, None, p_full)

            @pl.when(b != 0)
            def _():
                pick(ids)
                if phase:
                    grads(h, r, NSLOT, r * 8, p_plain.at[r])
                else:
                    probs(h, r, NSLOT, r * 8, extra, p_plain.at[r])

    def terms(u, j, m):
        ref = terms_of[u]
        at = [tab[r * nb + j * 4 + m] for r in range(4)]
        return (ref[at[0]] + ref[at[1]]) + (ref[at[2]] + ref[at[3]])

    def sum_copy(u, d, j):
        part = sums.at[u, d, pl.ds(j * 4, 4)]
        return rcopy(part, part, rs_s.at[u, d, j], rs_r.at[u, d, j], left if d else right)

    def add_own(u, d, j, first):
        @pl.loop(0, 4)
        def _(m):
            total = terms(u, j, m)
            if not first:
                total = total + sums[u, d, j * 4 + m].astype(jnp.float32)
            sums[u, d, j * 4 + m] = total.astype(jnp.bfloat16)

    def place(d, t):
        i = nz - 1 - z if d else z
        to = i + nz - 1 - t
        return i, nz - 1 - to if d else to

    def sum_step(u, t):
        for d in range(2):
            i, j = place(d, t)

            @pl.when(i == 0)
            def _():
                add_own(u, d, j, True)
                sum_copy(u, d, j).start()

            if t:
                @pl.when((i > 0) & (i <= t))
                def _():
                    sum_copy(u, d, j).wait_recv()
                    add_own(u, d, j, False)
                    sum_copy(u, d, j).start()

    def sum_sends(u):
        for t in range(nz - 1):
            for d in range(2):
                i, j = place(d, t)

                @pl.when(i <= t)
                def _():
                    sum_copy(u, d, j).wait_send()

    def finish(u):
        @pl.when(has_left)
        def _():
            sum_copy(u, 0, z).wait_recv()

        @pl.when(has_right)
        def _():
            sum_copy(u, 1, z).wait_recv()

        out = dk_out if u % 2 else dv_out
        mine = cols(core * 2 + u // 2)

        @pl.loop(0, 4)
        def _(m):
            total = terms(u, z, m)
            at_left = sums[u, 0, z * 4 + m].astype(jnp.float32)
            at_right = sums[u, 1, z * 4 + m].astype(jnp.float32)
            total = total + jnp.where(has_left, at_left, 0.0)
            total = total + jnp.where(has_right, at_right, 0.0)
            if u % 2:
                total = total * scale
            fin[u, m] = total.T.astype(jnp.bfloat16)

        for b in range(2):
            rcopy(
                fin.at[u, other * 2 + b], out.at[block(b), mine], out_s.at[u], out_r.at[u], partner
            ).start()
        for b in range(2):
            out[block(b), mine] = fin[u, core * 2 + b]

    def finish_all(u):
        part = fin.at[u, pl.ds(0, 2)]
        return rcopy(part, part, out_s.at[u], out_r.at[u], partner)

    def dq_back(h):
        for b in range(2):
            for g in range(GROUP):
                at = cols((core * 2 + h) * GROUP + g)
                rcopy(
                    dq_sc.at[h, other * 2 + b, g], dq_out.at[block(b), at],
                    dq_s.at[h], dq_r.at[h], partner,
                ).start()
        for b in range(2):
            for g in range(GROUP):
                at = cols((core * 2 + h) * GROUP + g)
                dq_out[block(b), at] = dq_sc[h, core * 2 + b, g]

    def dq_back_all(h):
        part = dq_sc.at[h, pl.ds(0, 2)]
        return rcopy(part, part, dq_s.at[h], dq_r.at[h], partner)

    def middle(fn, u):
        for dist in range(2, nz - 1):
            fn(u, dist)

    def last(u):
        if nz > 2:
            hop(u, nz - 1)

    def sum_middle(u):
        for t in range(1, nz - 2):
            sum_step(u, t)

    def sum_last(u):
        if nz > 2:
            sum_step(u, nz - 2)

    hop(0, 1)
    middle(hop, 0)
    send_own(1)
    last(0)
    hop(1, 1)
    for h in range(2):
        swap_q_all(h).wait_recv()
    for c in range(2):
        hand_off_all(0, c).wait_recv()
    hand_off(1)
    rows(0, 0, 0, 2)
    middle(hop, 1)
    send_own(2)
    rows(0, 0, 2, 4)
    last(1)
    hop(2, 1)
    sum_step(0, 0)
    rows(1, 0, 0, 2)
    middle(hop, 2)
    send_own(3)
    sum_middle(0)
    rows(1, 0, 2, 4)
    last(2)
    hop(3, 1)
    sum_last(0)
    sum_step(1, 0)
    dq_back(0)
    for c in range(2):
        hand_off_all(1, c).wait_recv()
    rows(0, 1, 0, 2)
    middle(hop, 3)
    sum_middle(1)
    rows(0, 1, 2, 4)
    last(3)
    sum_last(1)
    sum_step(2, 0)
    finish(0)
    rows(1, 1, 0, 2)
    sum_middle(2)
    rows(1, 1, 2, 4)
    sum_last(2)
    sum_step(3, 0)
    dq_back(1)
    finish(1)
    sum_middle(3)
    finish(2)
    sum_last(3)
    finish(3)

    for u in range(4):
        swap_kv_all(u).wait_send()
        hop_sends(u)
        sum_sends(u)
        finish_all(u).wait()
    for h in range(2):
        swap_q_all(h).wait_send()
        for c in range(2):
            hand_off_all(h, c).wait_send()
        dq_back_all(h).wait()


def per_device(n_seg, n_ctx, queries, keys, values, grad_slab, plan, random_blocks):
    nz = n_ctx // 2
    nb = nz * 4
    mb = plan[0]
    query_now = lax.dynamic_index_in_dim(queries[0], mb, 0, keepdims=False)
    key_now = lax.dynamic_index_in_dim(keys[0], mb, 0, keepdims=False)
    value_now = lax.dynamic_index_in_dim(values[0], mb, 0, keepdims=False)
    low = jnp.bfloat16
    vmem = pl.BlockSpec(memory_space=pltpu.VMEM)
    dma = pltpu.SemaphoreType.DMA
    rows4 = pltpu.VMEM((2, 4, GROUP, BLK, HD), low)
    line = pltpu.VMEM((nb, BLK, HD), low)
    tiles = pltpu.VMEM((32 + nb, BLK, HD), jnp.float32)
    wide = pltpu.VMEM((GROUP * BLK, nb * BLK), low)
    dq, dk, dv = pl.pallas_call(
        functools.partial(kernel, n_seg, nz),
        out_shape=(
            jax.ShapeDtypeStruct(query_now.shape, low),
            jax.ShapeDtypeStruct(key_now.shape, low),
            jax.ShapeDtypeStruct(value_now.shape, low),
        ),
        in_specs=[
            pl.BlockSpec(memory_space=pltpu.SMEM), vmem, pl.BlockSpec(memory_space=pl.ANY), vmem,
            vmem,
        ],
        out_specs=(vmem, vmem, vmem),
        scratch_shapes=[
            rows4, rows4, rows4, line, line, line, line, tiles, tiles, tiles, tiles,
            pltpu.VMEM((4, 2, nb, BLK, HD), low), pltpu.VMEM((4, 4, BLK, HD), low),
            pltpu.VMEM((nb * BLK, HD), low), pltpu.VMEM((nb * BLK, HD), low),
            pltpu.VMEM((GROUP * BLK, nb * BLK), jnp.float32), wide,
            pltpu.VMEM((4, GROUP * BLK, NSLOT * BLK), low), wide,
            pltpu.SMEM((4 * nb,), jnp.int32),
            dma((4,)), dma((4,)), dma((2,)), dma((2,)), dma((2, 2)), dma((2, 2)),
            dma((4, 2, nz)), dma((4, nz)), dma((4, 2, nz)), dma((4, 2, nz)),
            dma((2,)), dma((2,)), dma((4,)), dma((4,)),
        ],
        compiler_params=pltpu.CompilerParams(
            collective_id=0, has_side_effects=True, vmem_limit_bytes=60 * 1024 * 1024
        ),
        cost_estimate=pl.CostEstimate(
            flops=6_000_000_000, bytes_accessed=8_000_000, transcendentals=6_000_000
        ),
    )(random_blocks, query_now, grad_slab, key_now, value_now)
    return (dq[None], dk[None], dv[None])


def solution(mesh):
    return jax.shard_map(
        functools.partial(per_device, mesh.shape["segment"], mesh.shape["ctx"]),
        mesh=mesh,
        in_specs=(
            P("segment", None, "ctx", None),
            P("segment", None, "ctx", None),
            P("segment", None, "ctx", None),
            P("segment", "ctx", None),
            P("segment"),
            P(),
        ),
        out_specs=(P("segment", "ctx", None), P("segment", "ctx", None), P("segment", "ctx", None)),
        check_vma=False,
    )
```

time: 108 us -> 92 us (0.85)
  Pallas kernels: 90.7 us -> 81.1 us
  local copies, waits for them, and re-layouts: 14.2 us -> 9.28 us
    pallas_call x1, Pallas kernels: 90.7 us -> 81.1 us  [per_device(): pl.pallas_call(functools.partial(kernel, n_seg, nz), out_shape=(jax.Shape...]
    reshape x9 -> x0, local copies, waits for them, and re-layouts: 4.78 us -> none  [the longest x1 1.61 us: per_device(): query_grad = dq.transpose(1, 3, 0, 2, 4).reshape(1, 2 * BLK, -1)]
    transpose x5 -> x0, local copies, waits for them, and re-layouts: 4.47 us -> none  [the longest x1 2.09 us: per_device(): query_grad = dq.transpose(1, 3, 0, 2, 4).reshape(1, 2 * BLK, -1)]
    unnamed x3 -> x8, local copies, waits for them, and re-layouts: 0.76 us -> 5.12 us
    squeeze x0 -> x2, local copies, waits for them, and re-layouts: none -> 4.15 us  [the longest x1 2.3 us: per_device(): query_now = lax.dynamic_index_in_dim(queries[0], mb, 0, keepdims=False)]
    dynamic_slice x2 -> x0, local copies, waits for them, and re-layouts: 2.36 us -> none  [the longest x1 1.3 us: per_device(): query_now = lax.dynamic_index_in_dim(queries[0], mb, 0, keepdims=False)]
    another operation x1 -> x0, local copies, waits for them, and re-layouts: 1.78 us -> none  [per_device(): g_in = grad_slab[0].reshape(2, BLK, 4, GROUP, HD).transpose(2, 0, 3, 1, 4)]
where the time goes in v2:
time: 92 us; the launch traced here: 91.7 us
  Pallas kernels  81.1 us (88%)
  local copies, waits for them, and re-layouts  9.28 us (10%)
  between operations  1.31 us (1%)
    pallas_call x1, Pallas kernels, per_device(): pl.pallas_call(functools.partial(kernel, n_seg, nz), out_shape=(jax.Shape...  81.1 us
    unnamed x8, local copies, waits for them, and re-layouts  5.12 us
    squeeze x1, local copies, waits for them, and re-layouts, per_device(): query_now = lax.dynamic_index_in_dim(queries[0], mb, 0, keepdims=False)  2.3 us
    squeeze x1, local copies, waits for them, and re-layouts, per_device(): value_now = lax.dynamic_index_in_dim(values[0], mb, 0, keepdims=False)  1.85 us

profile of v2, /device:TPU:0, one launch (start us, length us, event | category | flops | bytes accessed | tf_op | source)
XLA Modules:
  0.0 91.7 jit_solution(11195203776833079612)
XLA Ops:
  1.3 1.4 %copy.9.rb_ref = s32[16,3]{1,0:T(8,128)} copy(s32[16,3]{0,1:T(4,128)} %param.11) | data formatting | bytes 384 | tf_op args[5]
  2.6 1.9 %dynamic-slice_bitcast_fusion.1 = (bf16[256,512]{1,0:T(8,128)(2,1)}, bf16[256,512]{1,0:T(8,128)(2,1)}) fusion(bf16[1,8,256,512]{3,2,1,0:T(8,128)(2,1)} %param.8, s32[]{:T(128)S(6)} %select_n.7, bf16[1,8,256,512]{3,2,1,0:T(8,128)(2,1)} %param.7), kind=kLoop, calls=%fused_computation.1 | loop fusion | bytes 1048580 | tf_op jit(solution)/shard_map/jit(dynamic_index_in_dim)/squeeze | solution.py:459
  4.5 2.3 %dynamic-slice_bitcast_fusion.q_in = bf16[256,2048]{1,0:T(8,128)(2,1)} fusion(bf16[1,8,256,2048]{3,2,1,0:T(8,128)(2,1)} %param.6, s32[]{:T(128)S(6)} %select_n.7), kind=kLoop, calls=%fused_computation | loop fusion | bytes 2097156 | tf_op jit(solution)/shard_map/jit(dynamic_index_in_dim)/squeeze | solution.py:457
  6.8 81.1 %shard_map.85 = (bf16[256,2048]{1,0:T(8,128)(2,1)}, bf16[256,512]{1,0:T(8,128)(2,1)}, bf16[256,512]{1,0:T(8,128)(2,1)}) custom-call(s32[16,3]{1,0:T(8,128)} %copy.9.rb_ref, bf16[256,2048]{1,0:T(8,128)(2,1)} %dynamic-slice_bitcast_fusion.q_in, bf16[1,256,2048]{2,1,0:T(8,128)(2,1)} %g_in.1, bf16[256,512]{1,0:T(8,128)(2,1)} %get-tuple-element.10.k_in, ...), custom_call_target="tpu_custom_call" | custom-call | flops 6000000000 | bytes 8000000 | tf_op jit(solution)/shard_map/pallas_call | solution.py:467
  87.9 0.0 copy-start.1
  87.9 0.0 copy-start
  87.9 2.4 %copy.14 = bf16[1,256,2048]{2,1,0:T(8,128)(2,1)} copy(bf16[1,256,2048]{2,1,0:T(8,128)(2,1)} %bitcast.13) | data formatting | bytes 2097152
  90.3 0.0 copy-done.1
  90.3 0.7 copy.15
  91.0 0.0 copy-done
  91.0 0.7 copy.16
Async XLA Ops:
  87.9 2.4 %copy-start.1 = (bf16[256,512]{1,0:T(8,128)(2,1)S(1)}, bf16[256,512]{1,0:T(8,128)(2,1)}, u32[]{:S(2)}) copy-start(bf16[256,512]{1,0:T(8,128)(2,1)} %get-tuple-element.7) | copy-start | bytes 786436
  87.9 3.1 %copy-start = (bf16[256,512]{1,0:T(8,128)(2,1)S(1)}, bf16[256,512]{1,0:T(8,128)(2,1)}, u32[]{:S(2)}) copy-start(bf16[256,512]{1,0:T(8,128)(2,1)} %get-tuple-element.8) | copy-start | bytes 786436

commit v3 on v2

--- a/solution.py
+++ b/solution.py
@@ -20,9 +20,9 @@
 
 
 def kernel(
-    n_seg, nz, rb_ref, q_in, g_in, k_in, v_in, dq_out, dk_out, dv_out,
+    n_seg, nz, rb_in, q_in, g_in, k_in, v_in, dq_out, dk_out, dv_out,
     q_sc, g_sc, dq_sc, k0, v0, k1, v1, slv0, slk0, slv1, slk1, sums, fin,
-    kgat, vgat, s_ref, dsb, p_plain, p_full, tab,
+    kgat, vgat, s_ref, dsb, p_plain, p_full, q_t, g_t, tab, rb_ref, rb_sem,
     swap_s, swap_r, qs_s, qs_r, grad_s, grad_r, ga_s, ga_r, rs_s, rs_r,
     dq_s, dq_r, out_s, out_r,
 ):
@@ -53,21 +53,21 @@
     def block(b):
         return pl.ds(b * BLK, BLK)
 
+    fetch = pltpu.make_async_copy(rb_in, rb_ref, rb_sem)
+    fetch.start()
+
     barrier = pltpu.get_barrier_semaphore()
     for dev in (
         partner, (ahead, z * 2), (ahead, z * 2 + 1), (behind, z * 2), (behind, z * 2 + 1)
     ):
         pl.semaphore_signal(barrier, inc=1, device_id=dev, device_id_type=MESH)
 
-    @pl.when(has_left)
-    def _():
-        pl.semaphore_signal(barrier, inc=1, device_id=left, device_id_type=MESH)
-
-    @pl.when(has_right)
-    def _():
-        pl.semaphore_signal(barrier, inc=1, device_id=right, device_id_type=MESH)
-
-    pl.semaphore_wait(barrier, 5 + has_left.astype(jnp.int32) + has_right.astype(jnp.int32))
+    for j in range(nz):
+        @pl.when(z != j)
+        def _():
+            pl.semaphore_signal(barrier, inc=1, device_id=(seg, j * 2 + core), device_id_type=MESH)
+
+    pl.semaphore_wait(barrier, nz + 4)
 
     def swap_kv(u):
         source = v_in if u % 2 else k_in
@@ -111,6 +111,24 @@
         part = line[u].at[pl.ds(j * 4, 4)]
         return rcopy(part, part, ga_s.at[u, d, j], ga_r.at[u, j], left if d else right)
 
+    def direct_copy(j):
+        part = line[0].at[pl.ds(z * 4, 4)]
+        return rcopy(part, part, ga_s.at[0, 0, j], ga_r.at[0, z], (seg, j * 2 + core))
+
+    def direct_in(j):
+        part = line[0].at[pl.ds(j * 4, 4)]
+        return rcopy(part, part, ga_s.at[0, 0, j], ga_r.at[0, j], (seg, j * 2 + core))
+
+    def by_distance(fn, dists):
+        for dist in dists:
+            @pl.when(z + dist < nz)
+            def _():
+                fn(z + dist)
+
+            @pl.when(z >= dist)
+            def _():
+                fn(z - dist)
+
     def send_own(u):
         swap_kv_all(u).wait_recv()
 
@@ -159,7 +177,8 @@
         for b in range(2):
             line[u][z * 4 + core * 2 + b] = source[block(b), cols(core * 2 + u // 2)]
         if u == 0:
-            send_own(0)
+            swap_kv_all(0).wait_recv()
+            by_distance(lambda j: direct_copy(j).start(), range(nz - 1, 0, -1))
     swap_q(1)
     for h in range(2):
         for b in range(2):
@@ -172,7 +191,7 @@
     def slots(r):
         b = z * 4 + r
         ids = [lax.rem(b + nb - 1, nb), b, lax.rem(b + 1, nb), 0]
-        ids += [rb_ref[b, i] for i in range(3)]
+        ids += [rb_ref[i, b] for i in range(3)]
         extra = (b != 0) & (b != 1) & (b != nb - 1)
         return b, ids, extra
 
@@ -185,18 +204,22 @@
             tab[r * nb + c] = jnp.where(b == 0, 32 + c, where)
         return 0
 
+    fetch.wait()
     lax.fori_loop(0, nb, fill, 0)
 
+    def turn(src, dst, h):
+        @pl.loop(0, 4)
+        def _(r):
+            dst[h, r] = src[h, r].reshape(GROUP * BLK, HD).T
+
     def chunk_loop(n, step):
-        size = 64
-        while size * n > 512 and size > 16:
-            size //= 2
+        size = 32 if n <= 8 else 16
 
         def run(i, _):
             step(pl.ds(pl.multiple_of(i * size, size), size))
             return 0
 
-        lax.fori_loop(0, GROUP * BLK // size, run, 0, unroll=2)
+        lax.fori_loop(0, GROUP * BLK // size, run, 0, unroll=4)
 
     def lanes(t):
         return slice(t * BLK, (t + 1) * BLK)
@@ -224,7 +247,7 @@
                 p_ref[at, lanes(t)] = ((exp_s[t] * shrink) * inverse).astype(jnp.bfloat16)
 
         chunk_loop(n, step)
-        dv = dot(g_sc[h, r].reshape(GROUP * BLK, HD).T, p_ref[:, :width], 1, 0)
+        dv = dot(g_t[h, r], p_ref[:, :width], 1, 0)
         for t in range(n):
             terms_of[2 * h][base + t] = dv[:, lanes(t)]
 
@@ -242,7 +265,7 @@
         chunk_loop(n, step)
         dq = dot(dsb[:, :width], kgat[:width], 1, 0) * scale
         dq_sc[h, r] = dq.astype(jnp.bfloat16).reshape(GROUP, BLK, HD)
-        dk = dot(q_sc[h, r].reshape(GROUP * BLK, HD).T, dsb[:, :width], 1, 0)
+        dk = dot(q_t[h, r], dsb[:, :width], 1, 0)
         for t in range(n):
             terms_of[2 * h + 1][base + t] = dk[:, lanes(t)]
 
@@ -322,14 +345,31 @@
                 def _():
                     sum_copy(u, d, j).wait_send()
 
+    def owner_copy(j):
+        return rcopy(
+            sums.at[3, 0, pl.ds(j * 4, 4)], sums.at[3, 1, pl.ds(z * 4, 4)],
+            rs_s.at[3, 0, j], rs_r.at[3, 1, z], (seg, j * 2 + core),
+        )
+
+    def owner_in(j):
+        part = sums.at[3, 1, pl.ds(j * 4, 4)]
+        return rcopy(part, part, rs_s.at[3, 0, j], rs_r.at[3, 1, j], (seg, j * 2 + core))
+
+    def to_owner(j):
+        add_own(3, 0, j, True)
+        owner_copy(j).start()
+
     def finish(u):
-        @pl.when(has_left)
-        def _():
-            sum_copy(u, 0, z).wait_recv()
-
-        @pl.when(has_right)
-        def _():
-            sum_copy(u, 1, z).wait_recv()
+        if u == 3:
+            by_distance(lambda j: owner_in(j).wait_recv(), range(1, nz))
+        else:
+            @pl.when(has_left)
+            def _():
+                sum_copy(u, 0, z).wait_recv()
+
+            @pl.when(has_right)
+            def _():
+                sum_copy(u, 1, z).wait_recv()
 
         out = dk_out if u % 2 else dv_out
         mine = cols(core * 2 + u // 2)
@@ -337,10 +377,12 @@
         @pl.loop(0, 4)
         def _(m):
             total = terms(u, z, m)
-            at_left = sums[u, 0, z * 4 + m].astype(jnp.float32)
-            at_right = sums[u, 1, z * 4 + m].astype(jnp.float32)
-            total = total + jnp.where(has_left, at_left, 0.0)
-            total = total + jnp.where(has_right, at_right, 0.0)
+            if u == 3:
+                parts = [(z != j, sums[3, 1, j * 4 + m]) for j in range(nz)]
+            else:
+                parts = [(has_left, sums[u, 0, z * 4 + m]), (has_right, sums[u, 1, z * 4 + m])]
+            for there, part in parts:
+                total = total + jnp.where(there, part.astype(jnp.float32), 0.0)
             if u % 2:
                 total = total * scale
             fin[u, m] = total.T.astype(jnp.bfloat16)
@@ -389,59 +431,63 @@
         if nz > 2:
             sum_step(u, nz - 2)
 
-    hop(0, 1)
-    middle(hop, 0)
+    by_distance(lambda j: direct_in(j).wait_recv(), [1])
     send_own(1)
-    last(0)
-    hop(1, 1)
     for h in range(2):
         swap_q_all(h).wait_recv()
+        turn(q_sc, q_t, h)
     for c in range(2):
         hand_off_all(0, c).wait_recv()
     hand_off(1)
+    turn(g_sc, g_t, 0)
+    by_distance(lambda j: direct_in(j).wait_recv(), range(2, nz))
+    hop(1, 1)
+    send_own(2)
     rows(0, 0, 0, 2)
     middle(hop, 1)
-    send_own(2)
+    hop(2, 1)
+    send_own(3)
     rows(0, 0, 2, 4)
     last(1)
-    hop(2, 1)
+    middle(hop, 2)
+    hop(3, 1)
     sum_step(0, 0)
     rows(1, 0, 0, 2)
-    middle(hop, 2)
-    send_own(3)
+    last(2)
+    middle(hop, 3)
+    rows(1, 0, 2, 4)
+    last(3)
     sum_middle(0)
-    rows(1, 0, 2, 4)
-    last(2)
-    hop(3, 1)
-    sum_last(0)
     sum_step(1, 0)
     dq_back(0)
     for c in range(2):
         hand_off_all(1, c).wait_recv()
+    turn(g_sc, g_t, 1)
     rows(0, 1, 0, 2)
-    middle(hop, 3)
+    sum_last(0)
+    rows(0, 1, 2, 4)
     sum_middle(1)
-    rows(0, 1, 2, 4)
-    last(3)
+    sum_step(2, 0)
+    rows(1, 1, 0, 2)
     sum_last(1)
-    sum_step(2, 0)
+    rows(1, 1, 2, 4)
+    by_distance(to_owner, range(nz - 1, 0, -1))
+    dq_back(1)
+    sum_middle(2)
     finish(0)
-    rows(1, 1, 0, 2)
-    sum_middle(2)
-    rows(1, 1, 2, 4)
     sum_last(2)
-    sum_step(3, 0)
-    dq_back(1)
     finish(1)
-    sum_middle(3)
     finish(2)
-    sum_last(3)
     finish(3)
 
+    by_distance(lambda j: direct_copy(j).wait_send(), range(1, nz))
+    by_distance(lambda j: owner_copy(j).wait_send(), range(1, nz))
     for u in range(4):
         swap_kv_all(u).wait_send()
-        hop_sends(u)
-        sum_sends(u)
+        if u:
+            hop_sends(u)
+        if u < 3:
+            sum_sends(u)
         finish_all(u).wait()
     for h in range(2):
         swap_q_all(h).wait_send()
@@ -450,17 +496,50 @@
         dq_back_all(h).wait()
 
 
+def move(pairs, sem):
+    copies = []
+    for i, (src, dst) in enumerate(pairs):
+        rows = src.shape[0] // 4
+        for n in range(4):
+            at = pl.ds(n * rows, rows)
+            copies.append(pltpu.make_async_copy(src.at[at], dst.at[at], sem.at[i, n]))
+    for copy in copies:
+        copy.start()
+    for copy in copies:
+        copy.wait()
+
+
+def pick_batch(plan_ref, q_all, k_all, v_all, q_out, k_out, v_out, sem):
+    mb = plan_ref[0]
+    sources = [ref.at[0, mb] for ref in (q_all, k_all, v_all)]
+    move(zip(sources, (q_out, k_out, v_out)), sem)
+
+
+def hand_out(dq_in, dk_in, dv_in, dq_out, dk_out, dv_out, sem):
+    targets = [ref.at[0] for ref in (dq_out, dk_out, dv_out)]
+    move(zip((dq_in, dk_in, dv_in), targets), sem)
+
+
 def per_device(n_seg, n_ctx, queries, keys, values, grad_slab, plan, random_blocks):
     nz = n_ctx // 2
     nb = nz * 4
-    mb = plan[0]
-    query_now = lax.dynamic_index_in_dim(queries[0], mb, 0, keepdims=False)
-    key_now = lax.dynamic_index_in_dim(keys[0], mb, 0, keepdims=False)
-    value_now = lax.dynamic_index_in_dim(values[0], mb, 0, keepdims=False)
     low = jnp.bfloat16
     vmem = pl.BlockSpec(memory_space=pltpu.VMEM)
+    hbm = pl.BlockSpec(memory_space=pl.ANY)
+    smem = pl.BlockSpec(memory_space=pltpu.SMEM)
     dma = pltpu.SemaphoreType.DMA
+    query_now, key_now, value_now = pl.pallas_call(
+        pick_batch,
+        out_shape=tuple(
+            jax.ShapeDtypeStruct(a.shape[2:], low) for a in (queries, keys, values)
+        ),
+        in_specs=[smem, hbm, hbm, hbm],
+        out_specs=(hbm, hbm, hbm),
+        scratch_shapes=[dma((3, 4))],
+        compiler_params=pltpu.CompilerParams(vmem_limit_bytes=60 * 1024 * 1024),
+    )(plan, queries, keys, values)
     rows4 = pltpu.VMEM((2, 4, GROUP, BLK, HD), low)
+    rows_t = pltpu.VMEM((2, 4, HD, GROUP * BLK), low)
     line = pltpu.VMEM((nb, BLK, HD), low)
     tiles = pltpu.VMEM((32 + nb, BLK, HD), jnp.float32)
     wide = pltpu.VMEM((GROUP * BLK, nb * BLK), low)
@@ -471,10 +550,7 @@
             jax.ShapeDtypeStruct(key_now.shape, low),
             jax.ShapeDtypeStruct(value_now.shape, low),
         ),
-        in_specs=[
-            pl.BlockSpec(memory_space=pltpu.SMEM), vmem, pl.BlockSpec(memory_space=pl.ANY), vmem,
-            vmem,
-        ],
+        in_specs=[hbm, vmem, hbm, vmem, vmem],
         out_specs=(vmem, vmem, vmem),
         scratch_shapes=[
             rows4, rows4, rows4, line, line, line, line, tiles, tiles, tiles, tiles,
@@ -482,7 +558,8 @@
             pltpu.VMEM((nb * BLK, HD), low), pltpu.VMEM((nb * BLK, HD), low),
             pltpu.VMEM((GROUP * BLK, nb * BLK), jnp.float32), wide,
             pltpu.VMEM((4, GROUP * BLK, NSLOT * BLK), low), wide,
-            pltpu.SMEM((4 * nb,), jnp.int32),
+            rows_t, rows_t, pltpu.SMEM((4 * nb,), jnp.int32),
+            pltpu.SMEM(random_blocks.shape[::-1], jnp.int32), dma,
             dma((4,)), dma((4,)), dma((2,)), dma((2,)), dma((2, 2)), dma((2, 2)),
             dma((4, 2, nz)), dma((4, nz)), dma((4, 2, nz)), dma((4, 2, nz)),
             dma((2,)), dma((2,)), dma((4,)), dma((4,)),
@@ -493,8 +570,16 @@
         cost_estimate=pl.CostEstimate(
             flops=6_000_000_000, bytes_accessed=8_000_000, transcendentals=6_000_000
         ),
-    )(random_blocks, query_now, grad_slab, key_now, value_now)
-    return (dq[None], dk[None], dv[None])
+    )(random_blocks.T, query_now, grad_slab, key_now, value_now)
+    outs = (dq, dk, dv)
+    return pl.pallas_call(
+        hand_out,
+        out_shape=tuple(jax.ShapeDtypeStruct((1,) + a.shape, low) for a in outs),
+        in_specs=[hbm, hbm, hbm],
+        out_specs=(hbm, hbm, hbm),
+        scratch_shapes=[dma((3, 4))],
+        compiler_params=pltpu.CompilerParams(vmem_limit_bytes=60 * 1024 * 1024),
+    )(*outs)
 
 
 def solution(mesh):

time: 92 us -> 189 us (2.05)
  Pallas kernels: 81.1 us -> 186 us
  local copies, waits for them, and re-layouts: 9.28 us -> 0 us
    pallas_call x0 -> x2, Pallas kernels: none -> 97.7 us  [the longest x1 48.9 us: per_device(): pl.pallas_call(hand_out, out_shape=tuple((jax.ShapeDtypeStruct((1,) + a.s...]
    pallas_call x1, Pallas kernels: 81.1 us -> 88.7 us  [per_device(): pl.pallas_call(functools.partial(kernel, n_seg, nz), out_shape=(jax.Shape...]
    unnamed x8 -> x0, local copies, waits for them, and re-layouts: 5.12 us -> none
    squeeze x2 -> x0, local copies, waits for them, and re-layouts: 4.15 us -> none  [the longest x1 2.3 us: per_device(): query_now = lax.dynamic_index_in_dim(queries[0], mb, 0, keepdims=False)]
where the time goes in v3:
time: 189 us; the launch traced here: 188 us
  Pallas kernels  186 us (98%)
    pallas_call x1, Pallas kernels, per_device(): pl.pallas_call(functools.partial(kernel, n_seg, nz), out_shape=(jax.Shape...  88.7 us
    pallas_call x1, Pallas kernels, per_device(): pl.pallas_call(hand_out, out_shape=tuple((jax.ShapeDtypeStruct((1,) + a.s...  48.9 us
    pallas_call x1, Pallas kernels, per_device(): pl.pallas_call(pick_batch, out_shape=tuple((jax.ShapeDtypeStruct(a.shape[...  48.9 us

profile of v3, /device:TPU:0, one launch (start us, length us, event | category | flops | bytes accessed | tf_op | source)
XLA Modules:
  0.0 187.9 jit_solution(5904323751785431712)
XLA Ops:
  1.3 48.9 %shard_map.85 = (bf16[256,2048]{1,0:T(8,128)(2,1)}, bf16[256,512]{1,0:T(8,128)(2,1)}, bf16[256,512]{1,0:T(8,128)(2,1)}) custom-call(s32[1]{0:T(128)S(6)} %copy.9.plan_ref, bf16[1,8,256,2048]{3,2,1,0:T(8,128)(2,1)} %q_all.1, bf16[1,8,256,512]{3,2,1,0:T(8,128)(2,1)} %k_all.1, bf16[1,8,256,512]{3,2,1,0:T(8,128)(2,1)} %v_all.1), custom_call_target="tpu_custom_call" | custom-call | tf_op jit(solution)/shard_map/pallas_call | solution.py:531
  50.1 88.7 %shard_map.86 = (bf16[256,2048]{1,0:T(8,128)(2,1)}, bf16[256,512]{1,0:T(8,128)(2,1)}, bf16[256,512]{1,0:T(8,128)(2,1)}) custom-call(s32[3,16]{1,0:T(4,128)} %bitcast.1, bf16[256,2048]{1,0:T(8,128)(2,1)} %get-tuple-element.9.q_in, bf16[1,256,2048]{2,1,0:T(8,128)(2,1)} %g_in.1, bf16[256,512]{1,0:T(8,128)(2,1)} %get-tuple-element.10.k_in, ...), custom_call_target="tpu_custom_call" | custom-call | flops 6000000000 | bytes 8000000 | tf_op jit(solution)/shard_map/pallas_call | solution.py:546
  138.8 48.9 %shard_map.87 = (bf16[1,256,2048]{2,1,0:T(8,128)(2,1)}, bf16[1,256,512]{2,1,0:T(8,128)(2,1)}, bf16[1,256,512]{2,1,0:T(8,128)(2,1)}) custom-call(bf16[256,2048]{1,0:T(8,128)(2,1)} %get-tuple-element.12.dq_in, bf16[256,512]{1,0:T(8,128)(2,1)} %get-tuple-element.13.dk_in, bf16[256,512]{1,0:T(8,128)(2,1)} %get-tuple-element.14.dv_in), custom_call_target="tpu_custom_call" | custom-call | tf_op jit(solution)/shard_map/pallas_call | solution.py:575

commit v4 on v2

--- a/solution.py
+++ b/solution.py
@@ -20,9 +20,10 @@
 
 
 def kernel(
-    n_seg, nz, rb_ref, q_in, g_in, k_in, v_in, dq_out, dk_out, dv_out,
+    n_seg, nz, rb_in, q_in, g_in, k_in, v_in, dq_out, dk_out, dv_out,
     q_sc, g_sc, dq_sc, k0, v0, k1, v1, slv0, slk0, slv1, slk1, sums, fin,
-    kgat, vgat, s_ref, dsb, p_plain, p_full, tab,
+    kgat, vgat, s_ref, p_plain, p_full, q_t, g_t, q_own, g_own, kv_own, dq_box, tab, rb_ref,
+    rb_sem,
     swap_s, swap_r, qs_s, qs_r, grad_s, grad_r, ga_s, ga_r, rs_s, rs_r,
     dq_s, dq_r, out_s, out_r,
 ):
@@ -50,8 +51,14 @@
     def cols(at):
         return pl.ds(pl.multiple_of(at * HD, HD), HD)
 
+    def lanes(t):
+        return slice(t * BLK, (t + 1) * BLK)
+
     def block(b):
         return pl.ds(b * BLK, BLK)
+
+    fetch = pltpu.make_async_copy(rb_in, rb_ref, rb_sem)
+    fetch.start()
 
     barrier = pltpu.get_barrier_semaphore()
     for dev in (
@@ -69,25 +76,29 @@
 
     pl.semaphore_wait(barrier, 5 + has_left.astype(jnp.int32) + has_right.astype(jnp.int32))
 
+    for b in range(2):
+        for j in range(4):
+            kv_own[0, j, b] = k_in[block(b), lanes(j)]
+            kv_own[1, j, b] = v_in[block(b), lanes(j)]
+            for g in range(GROUP):
+                g_own[j, b, g] = g_in[0, block(b), lanes(j * GROUP + g)]
+                q_own[j, b, g] = q_in[block(b), lanes(j * GROUP + g)]
+
     def swap_kv(u):
-        source = v_in if u % 2 else k_in
-        for b in range(2):
-            rcopy(
-                source.at[block(b), cols(other * 2 + u // 2)], line[u].at[z * 4 + core * 2 + b],
-                swap_s.at[u], swap_r.at[u], partner,
-            ).start()
+        return rcopy(
+            kv_own.at[u % 2, other * 2 + u // 2], line[u].at[pl.ds(z * 4 + core * 2, 2)],
+            swap_s.at[u], swap_r.at[u], partner,
+        )
 
     def swap_kv_all(u):
         part = line[u].at[pl.ds(z * 4 + other * 2, 2)]
         return rcopy(part, part, swap_s.at[u], swap_r.at[u], partner)
 
     def swap_q(h):
-        for b in range(2):
-            for g in range(GROUP):
-                rcopy(
-                    q_in.at[block(b), cols((other * 2 + h) * GROUP + g)],
-                    q_sc.at[h, core * 2 + b, g], qs_s.at[h], qs_r.at[h], partner,
-                ).start()
+        return rcopy(
+            q_own.at[other * 2 + h], q_sc.at[h, pl.ds(core * 2, 2)],
+            qs_s.at[h], qs_r.at[h], partner,
+        )
 
     def swap_q_all(h):
         part = q_sc.at[h, pl.ds(other * 2, 2)]
@@ -95,13 +106,10 @@
 
     def hand_off(h):
         for c in range(2):
-            for b in range(2):
-                for g in range(GROUP):
-                    rcopy(
-                        g_in.at[0, block(b), cols((c * 2 + h) * GROUP + g)],
-                        g_sc.at[h, core * 2 + b, g],
-                        grad_s.at[h, c], grad_r.at[h, core], (behind, z * 2 + c),
-                    ).start()
+            rcopy(
+                g_own.at[c * 2 + h], g_sc.at[h, pl.ds(core * 2, 2)],
+                grad_s.at[h, c], grad_r.at[h, core], (behind, z * 2 + c),
+            ).start()
 
     def hand_off_all(h, c):
         part = g_sc.at[h, pl.ds(c * 2, 2)]
@@ -149,22 +157,18 @@
             def _():
                 chunk_copy(u, 1, z + dist).wait_send()
 
-    swap_kv(0)
+    swap_kv(0).start()
     hand_off(0)
-    swap_q(0)
+    swap_q(0).start()
     for u in range(4):
-        source = v_in if u % 2 else k_in
         if u:
-            swap_kv(u)
-        for b in range(2):
-            line[u][z * 4 + core * 2 + b] = source[block(b), cols(core * 2 + u // 2)]
+            swap_kv(u).start()
+        line[u][pl.ds(z * 4 + core * 2, 2)] = kv_own[u % 2, core * 2 + u // 2]
         if u == 0:
             send_own(0)
-    swap_q(1)
+    swap_q(1).start()
     for h in range(2):
-        for b in range(2):
-            for g in range(GROUP):
-                q_sc[h, core * 2 + b, g] = q_in[block(b), cols((core * 2 + h) * GROUP + g)]
+        q_sc[h, pl.ds(core * 2, 2)] = q_own[core * 2 + h]
 
     for u in range(4):
         terms_of[u][NSLOT] = jnp.zeros((BLK, HD), jnp.float32)
@@ -172,7 +176,7 @@
     def slots(r):
         b = z * 4 + r
         ids = [lax.rem(b + nb - 1, nb), b, lax.rem(b + 1, nb), 0]
-        ids += [rb_ref[b, i] for i in range(3)]
+        ids += [rb_ref[i, b] for i in range(3)]
         extra = (b != 0) & (b != 1) & (b != nb - 1)
         return b, ids, extra
 
@@ -185,7 +189,13 @@
             tab[r * nb + c] = jnp.where(b == 0, 32 + c, where)
         return 0
 
+    fetch.wait()
     lax.fori_loop(0, nb, fill, 0)
+
+    def turn(src, dst, h):
+        @pl.loop(0, 4)
+        def _(r):
+            dst[h, r] = src[h, r].reshape(GROUP * BLK, HD).T
 
     def chunk_loop(n, step):
         size = 64
@@ -197,9 +207,6 @@
             return 0
 
         lax.fori_loop(0, GROUP * BLK // size, run, 0, unroll=2)
-
-    def lanes(t):
-        return slice(t * BLK, (t + 1) * BLK)
 
     def total_of(tiles):
         tiles = list(tiles)
@@ -224,7 +231,7 @@
                 p_ref[at, lanes(t)] = ((exp_s[t] * shrink) * inverse).astype(jnp.bfloat16)
 
         chunk_loop(n, step)
-        dv = dot(g_sc[h, r].reshape(GROUP * BLK, HD).T, p_ref[:, :width], 1, 0)
+        dv = dot(g_t[h, r], p_ref[:, :width], 1, 0)
         for t in range(n):
             terms_of[2 * h][base + t] = dv[:, lanes(t)]
 
@@ -237,12 +244,12 @@
             p = [p_ref[at, lanes(t)].astype(jnp.float32) for t in range(n)]
             delta = total_of([a * b for a, b in zip(p, dp)])
             for t in range(n):
-                dsb[at, lanes(t)] = (p[t] * (dp[t] - delta)).astype(jnp.bfloat16)
+                p_ref[at, lanes(t)] = (p[t] * (dp[t] - delta)).astype(jnp.bfloat16)
 
         chunk_loop(n, step)
-        dq = dot(dsb[:, :width], kgat[:width], 1, 0) * scale
+        dq = dot(p_ref[:, :width], kgat[:width], 1, 0) * scale
         dq_sc[h, r] = dq.astype(jnp.bfloat16).reshape(GROUP, BLK, HD)
-        dk = dot(q_sc[h, r].reshape(GROUP * BLK, HD).T, dsb[:, :width], 1, 0)
+        dk = dot(q_t[h, r], p_ref[:, :width], 1, 0)
         for t in range(n):
             terms_of[2 * h + 1][base + t] = dk[:, lanes(t)]
 
@@ -357,18 +364,21 @@
         return rcopy(part, part, out_s.at[u], out_r.at[u], partner)
 
     def dq_back(h):
-        for b in range(2):
-            for g in range(GROUP):
-                at = cols((core * 2 + h) * GROUP + g)
-                rcopy(
-                    dq_sc.at[h, other * 2 + b, g], dq_out.at[block(b), at],
-                    dq_s.at[h], dq_r.at[h], partner,
-                ).start()
+        rcopy(
+            dq_sc.at[h, pl.ds(other * 2, 2)], dq_box.at[h], dq_s.at[h], dq_r.at[h], partner
+        ).start()
         for b in range(2):
             for g in range(GROUP):
                 at = cols((core * 2 + h) * GROUP + g)
                 dq_out[block(b), at] = dq_sc[h, core * 2 + b, g]
 
+    def dq_in(h):
+        dq_back_all(h).wait()
+        for b in range(2):
+            for g in range(GROUP):
+                at = cols((other * 2 + h) * GROUP + g)
+                dq_out[block(b), at] = dq_box[h, b, g]
+
     def dq_back_all(h):
         part = dq_sc.at[h, pl.ds(0, 2)]
         return rcopy(part, part, dq_s.at[h], dq_r.at[h], partner)
@@ -390,15 +400,18 @@
             sum_step(u, nz - 2)
 
     hop(0, 1)
+    for h in range(2):
+        swap_q_all(h).wait_recv()
+    turn(q_sc, q_t, 0)
     middle(hop, 0)
     send_own(1)
+    turn(q_sc, q_t, 1)
     last(0)
     hop(1, 1)
-    for h in range(2):
-        swap_q_all(h).wait_recv()
     for c in range(2):
         hand_off_all(0, c).wait_recv()
     hand_off(1)
+    turn(g_sc, g_t, 0)
     rows(0, 0, 0, 2)
     middle(hop, 1)
     send_own(2)
@@ -418,6 +431,7 @@
     dq_back(0)
     for c in range(2):
         hand_off_all(1, c).wait_recv()
+    turn(g_sc, g_t, 1)
     rows(0, 1, 0, 2)
     middle(hop, 3)
     sum_middle(1)
@@ -433,8 +447,10 @@
     sum_step(3, 0)
     dq_back(1)
     finish(1)
+    dq_in(0)
     sum_middle(3)
     finish(2)
+    dq_in(1)
     sum_last(3)
     finish(3)
 
@@ -447,20 +463,50 @@
         swap_q_all(h).wait_send()
         for c in range(2):
             hand_off_all(h, c).wait_send()
-        dq_back_all(h).wait()
+
+
+def pick_batch(plan_ref, q_all, k_all, v_all, q_out, k_out, v_out, sem):
+    mb = plan_ref[0]
+    copies = []
+    for i, (src, dst) in enumerate(((q_all, q_out), (k_all, k_out), (v_all, v_out))):
+        rows = dst.shape[0] // 4
+        for n in range(4):
+            at = pl.ds(n * rows, rows)
+            copies.append(pltpu.make_async_copy(src.at[0, mb, at], dst.at[at], sem.at[i, n]))
+    for copy in copies:
+        copy.start()
+    for copy in copies:
+        copy.wait()
+
+
+def hand_out(dq_in, dk_in, dv_in, dq_out, dk_out, dv_out):
+    dq_out[0] = dq_in[...]
+    dk_out[0] = dk_in[...]
+    dv_out[0] = dv_in[...]
 
 
 def per_device(n_seg, n_ctx, queries, keys, values, grad_slab, plan, random_blocks):
     nz = n_ctx // 2
     nb = nz * 4
-    mb = plan[0]
-    query_now = lax.dynamic_index_in_dim(queries[0], mb, 0, keepdims=False)
-    key_now = lax.dynamic_index_in_dim(keys[0], mb, 0, keepdims=False)
-    value_now = lax.dynamic_index_in_dim(values[0], mb, 0, keepdims=False)
     low = jnp.bfloat16
     vmem = pl.BlockSpec(memory_space=pltpu.VMEM)
+    hbm = pl.BlockSpec(memory_space=pl.ANY)
+    smem = pl.BlockSpec(memory_space=pltpu.SMEM)
     dma = pltpu.SemaphoreType.DMA
+    roomy = pltpu.CompilerParams(vmem_limit_bytes=60 * 1024 * 1024)
+    query_now, key_now, value_now = pl.pallas_call(
+        pick_batch,
+        out_shape=tuple(
+            jax.ShapeDtypeStruct(a.shape[2:], low) for a in (queries, keys, values)
+        ),
+        in_specs=[smem, hbm, hbm, hbm],
+        out_specs=(vmem, vmem, vmem),
+        scratch_shapes=[dma((3, 4))],
+        compiler_params=roomy,
+    )(plan, queries, keys, values)
     rows4 = pltpu.VMEM((2, 4, GROUP, BLK, HD), low)
+    rows_t = pltpu.VMEM((2, 4, HD, GROUP * BLK), low)
+    heads = pltpu.VMEM((4, 2, GROUP, BLK, HD), low)
     line = pltpu.VMEM((nb, BLK, HD), low)
     tiles = pltpu.VMEM((32 + nb, BLK, HD), jnp.float32)
     wide = pltpu.VMEM((GROUP * BLK, nb * BLK), low)
@@ -471,18 +517,18 @@
             jax.ShapeDtypeStruct(key_now.shape, low),
             jax.ShapeDtypeStruct(value_now.shape, low),
         ),
-        in_specs=[
-            pl.BlockSpec(memory_space=pltpu.SMEM), vmem, pl.BlockSpec(memory_space=pl.ANY), vmem,
-            vmem,
-        ],
+        in_specs=[hbm, vmem, vmem, vmem, vmem],
         out_specs=(vmem, vmem, vmem),
         scratch_shapes=[
             rows4, rows4, rows4, line, line, line, line, tiles, tiles, tiles, tiles,
             pltpu.VMEM((4, 2, nb, BLK, HD), low), pltpu.VMEM((4, 4, BLK, HD), low),
             pltpu.VMEM((nb * BLK, HD), low), pltpu.VMEM((nb * BLK, HD), low),
-            pltpu.VMEM((GROUP * BLK, nb * BLK), jnp.float32), wide,
+            pltpu.VMEM((GROUP * BLK, nb * BLK), jnp.float32),
             pltpu.VMEM((4, GROUP * BLK, NSLOT * BLK), low), wide,
+            rows_t, rows_t, heads, heads, pltpu.VMEM((2, 4, 2, BLK, HD), low),
+            pltpu.VMEM((2, 2, GROUP, BLK, HD), low),
             pltpu.SMEM((4 * nb,), jnp.int32),
+            pltpu.SMEM(random_blocks.shape[::-1], jnp.int32), dma,
             dma((4,)), dma((4,)), dma((2,)), dma((2,)), dma((2, 2)), dma((2, 2)),
             dma((4, 2, nz)), dma((4, nz)), dma((4, 2, nz)), dma((4, 2, nz)),
             dma((2,)), dma((2,)), dma((4,)), dma((4,)),
@@ -493,8 +539,15 @@
         cost_estimate=pl.CostEstimate(
             flops=6_000_000_000, bytes_accessed=8_000_000, transcendentals=6_000_000
         ),
-    )(random_blocks, query_now, grad_slab, key_now, value_now)
-    return (dq[None], dk[None], dv[None])
+    )(random_blocks.T, query_now, grad_slab, key_now, value_now)
+    outs = (dq, dk, dv)
+    return pl.pallas_call(
+        hand_out,
+        out_shape=tuple(jax.ShapeDtypeStruct((1,) + a.shape, low) for a in outs),
+        in_specs=[vmem, vmem, vmem],
+        out_specs=(vmem, vmem, vmem),
+        compiler_params=roomy,
+    )(*outs)
 
 
 def solution(mesh):

time: 92 us -> 91.1 us (level)
  local copies, waits for them, and re-layouts: 9.28 us -> 0 us
  Pallas kernels: 81.1 us -> 88.9 us
    unnamed x8 -> x0, local copies, waits for them, and re-layouts: 5.12 us -> none
    pallas_call x0 -> x2, Pallas kernels: none -> 5.03 us  [the longest x1 2.53 us: per_device(): pl.pallas_call(pick_batch, out_shape=tuple((jax.ShapeDtypeStruct(a.shape[...]
    squeeze x2 -> x0, local copies, waits for them, and re-layouts: 4.15 us -> none  [the longest x1 2.3 us: per_device(): query_now = lax.dynamic_index_in_dim(queries[0], mb, 0, keepdims=False)]
    pallas_call x1, Pallas kernels: 81.1 us -> 83.8 us  [per_device(): pl.pallas_call(functools.partial(kernel, n_seg, nz), out_shape=(jax.Shape...]
where the time goes in v4:
time: 91.1 us; the launch traced here: 90.2 us
  Pallas kernels  88.9 us (98%)
  between operations  1.29 us (1%)
    pallas_call x1, Pallas kernels, per_device(): pl.pallas_call(functools.partial(kernel, n_seg, nz), out_shape=(jax.Shape...  83.8 us
    pallas_call x1, Pallas kernels, per_device(): pl.pallas_call(pick_batch, out_shape=tuple((jax.ShapeDtypeStruct(a.shape[...  2.53 us
    pallas_call x1, Pallas kernels, per_device(): pl.pallas_call(hand_out, out_shape=tuple((jax.ShapeDtypeStruct((1,) + a.s...  2.5 us

profile of v4, /device:TPU:0, one launch (start us, length us, event | category | flops | bytes accessed | tf_op | source)
XLA Modules:
  0.0 90.2 jit_solution(14709332617704248074)
XLA Ops:
  1.3 2.5 %shard_map.85 = (bf16[256,2048]{1,0:T(8,128)(2,1)}, bf16[256,512]{1,0:T(8,128)(2,1)}, bf16[256,512]{1,0:T(8,128)(2,1)}) custom-call(s32[1]{0:T(128)S(6)} %copy.9.plan_ref, bf16[1,8,256,2048]{3,2,1,0:T(8,128)(2,1)} %q_all.1, bf16[1,8,256,512]{3,2,1,0:T(8,128)(2,1)} %k_all.1, bf16[1,8,256,512]{3,2,1,0:T(8,128)(2,1)} %v_all.1), custom_call_target="tpu_custom_call" | custom-call | tf_op jit(solution)/shard_map/pallas_call | solution.py:497
  3.8 83.8 %shard_map.86 = (bf16[256,2048]{1,0:T(8,128)(2,1)}, bf16[256,512]{1,0:T(8,128)(2,1)}, bf16[256,512]{1,0:T(8,128)(2,1)}) custom-call(s32[3,16]{1,0:T(4,128)} %bitcast.1, bf16[256,2048]{1,0:T(8,128)(2,1)} %get-tuple-element.9.q_in, bf16[1,256,2048]{2,1,0:T(8,128)(2,1)} %g_in.1, bf16[256,512]{1,0:T(8,128)(2,1)} %get-tuple-element.10.k_in, ...), custom_call_target="tpu_custom_call" | custom-call | flops 6000000000 | bytes 8000000 | tf_op jit(solution)/shard_map/pallas_call | solution.py:513
  87.7 2.5 %shard_map.87 = (bf16[1,256,2048]{2,1,0:T(8,128)(2,1)}, bf16[1,256,512]{2,1,0:T(8,128)(2,1)}, bf16[1,256,512]{2,1,0:T(8,128)(2,1)}) custom-call(bf16[256,2048]{1,0:T(8,128)(2,1)} %get-tuple-element.12.dq_in, bf16[256,512]{1,0:T(8,128)(2,1)} %get-tuple-element.13.dk_in, bf16[256,512]{1,0:T(8,128)(2,1)} %get-tuple-element.14.dv_in), custom_call_target="tpu_custom_call" | custom-call | tf_op jit(solution)/shard_map/pallas_call | solution.py:544
